TPU v7x, 256 devices: a whole 4x4x8 slice. The times are simulated.
256 devices in a mesh: seq: 32 (over z, x), head: 8 (over y, core).
Axes of the slice: x: 4, y: 4, z: 8, core: 2. Of those that a mesh axis runs over, the one named last changes fastest.
Arguments:
- queries: bfloat16 [32768, 4096], P('seq', 'head'), may hold values from -4 to 4
- keys: bfloat16 [32768, 4096], P('seq', 'head'), may hold values from -4 to 4
- values: bfloat16 [32768, 4096], P('seq', 'head'), may hold values from -100 to 100
- gain: float32 [4096], P('head'), may hold values from 0.5 to 1.5
- grad_out: bfloat16 [32768, 4096], P('seq', 'head'), may hold values from -100 to 100
Outputs:
- normed: bfloat16 [32768, 4096], P('seq', 'head')
- grad_queries: bfloat16 [32768, 4096], P('seq', 'head')
- grad_keys: bfloat16 [32768, 4096], P('seq', 'head')
- grad_values: bfloat16 [32768, 4096], P('seq', 'head')
All inputs are finite; a program needn't handle non-finite values.
Results may differ from a plain program's by a relative error of at most 0.0058.
Values sent between devices are 32-bit elements; how exact they have to be, the bound alone decides.
A program may use at most 128 MiB of HBM per device.

v0:
```python
import jax
import jax.numpy as jnp
from jax import lax
from jax.sharding import PartitionSpec as P

HD = 128
BLK = 512


EPS = 1e-06


def passed_along(block, axis, distance):
    devices = range(lax.axis_size(axis))
    route = [(i - distance, i) for i in devices if i - distance in devices]
    return lax.ppermute(block, axis, route)


def shards(queries, keys, values, gain, grad_out):
    f32 = jnp.float32
    bf16 = jnp.bfloat16
    rows, width = queries.shape
    heads = width // HD
    blocks = rows // BLK
    total_width = width * lax.axis_size("head")
    shape4 = (blocks, BLK, heads, HD)
    qs = queries.reshape(shape4)
    ks = keys.reshape(shape4)
    vs = values.reshape(shape4)
    mask = jnp.arange(BLK)[None, :] <= jnp.arange(BLK)[:, None]
    zero_state = jnp.zeros((heads, HD, HD), f32)
    scores = jnp.einsum("bshd,bthd->bhst", qs, ks, preferred_element_type=f32)
    a_bf = jnp.where(mask, scores, 0.0).astype(bf16)
    block_kv = jnp.einsum("bthd,bthe->bhde", ks, vs, preferred_element_type=f32)
    local_kv = jnp.sum(block_kv, axis=0)

    def pass_lower(step, carry):
        moving, accum = carry
        moving = passed_along(moving, "seq", 1)
        return (moving, accum + moving)

    _, incoming = lax.fori_loop(0, lax.axis_size("seq") - 1, pass_lower, (local_kv, zero_state))
    earlier = incoming[None] + jnp.cumsum(block_kv, axis=0) - block_kv
    state_bf = earlier.astype(bf16)
    num = jnp.einsum("bhst,bthe->bshe", a_bf, vs, preferred_element_type=f32)
    num = num + jnp.einsum("bshd,bhde->bshe", qs, state_bf, preferred_element_type=f32)
    gains = gain.reshape(heads, HD)
    scaled = grad_out.astype(f32).reshape(shape4) * gains
    squares, products = lax.psum(
        (jnp.sum(num * num, axis=(2, 3)), jnp.sum(scaled * num, axis=(2, 3))), "head"
    )
    ratio = lax.rsqrt(squares / total_width + EPS)[:, :, None, None]
    normed = (num * ratio * gains).astype(bf16).reshape(rows, width)
    inner = (products / total_width)[:, :, None, None]
    dnum = (ratio * (scaled - ratio * ratio * inner * num)).astype(bf16)
    block_qd = jnp.einsum("bshd,bshe->bhde", qs, dnum, preferred_element_type=f32)
    local_qd = jnp.sum(block_qd, axis=0)

    def pass_upper(step, carry):
        moving, accum = carry
        moving = passed_along(moving, "seq", -1)
        return (moving, accum + moving)

    _, arriving = lax.fori_loop(0, lax.axis_size("seq") - 1, pass_upper, (local_qd, zero_state))
    later = arriving[None] + local_qd[None] - jnp.cumsum(block_qd, axis=0)
    later_bf = later.astype(bf16)
    bmat = jnp.einsum("bshe,bthe->bhst", dnum, vs, preferred_element_type=f32)
    bmat = jnp.where(mask, bmat, 0.0).astype(bf16)
    grad_q = jnp.einsum("bhst,bthd->bshd", bmat, ks, preferred_element_type=f32)
    grad_q = grad_q + jnp.einsum("bshe,bhde->bshd", dnum, state_bf, preferred_element_type=f32)
    grad_k = jnp.einsum("bhst,bshd->bthd", bmat, qs, preferred_element_type=f32)
    grad_k = grad_k + jnp.einsum("bthe,bhde->bthd", vs, later_bf, preferred_element_type=f32)
    grad_v = jnp.einsum("bhst,bshe->bthe", a_bf, dnum, preferred_element_type=f32)
    grad_v = grad_v + jnp.einsum("bthd,bhde->bthe", ks, later_bf, preferred_element_type=f32)
    return (
        normed,
        grad_q.astype(bf16).reshape(rows, width),
        grad_k.astype(bf16).reshape(rows, width),
        grad_v.astype(bf16).reshape(rows, width),
    )


def solution(mesh):
    return jax.shard_map(
        shards,
        mesh=mesh,
        in_specs=(
            P("seq", "head"),
            P("seq", "head"),
            P("seq", "head"),
            P("head"),
            P("seq", "head"),
        ),
        out_specs=(P("seq", "head"), P("seq", "head"), P("seq", "head"), P("seq", "head")),
        check_vma=False,
    )
```

profile of v0, /device:TPU:102, one launch (start us, length us, event | category | flops | bytes accessed | tf_op | source)
XLA Modules:
  0.0 896.8 jit_solution(13472258940530614630)
XLA Ops:
  6.9 454.3 %while.26 = (s32[]{:T(128)}, f32[4,128,128]{2,1,0:T(8,128)}, f32[4,128,128]{2,1,0:T(8,128)}, s32[]{:T(128)}, s32[]{:T(128)}) while((s32[]{:T(128)}, f32[4,128,128]{2,1,0:T(8,128)}, f32[4,128,128]{2,1,0:T(8,128)}, s32[]{:T(128)}, s32[]{:T(128)}) %tuple.52), condition=%wide.region_2.3_spmd.clone, body=%wide.region_1.2_spmd.clone.sunk | while | flops 131075 | bytes 2359407 | solution.py:42
  19.3 7.6 collective-permute-start
  34.2 7.6 collective-permute-start
  48.4 7.6 collective-permute-start
  62.6 7.6 collective-permute-start
  76.7 7.6 collective-permute-start
  90.9 7.6 collective-permute-start
  105.1 7.6 collective-permute-start
  119.3 7.6 collective-permute-start
  133.4 7.6 collective-permute-start
  148.3 7.6 collective-permute-start
  164.3 7.6 collective-permute-start
  181.1 7.6 collective-permute-start
  197.0 7.6 collective-permute-start
  212.1 7.6 collective-permute-start
  226.3 7.6 collective-permute-start
  240.5 7.6 collective-permute-start
  254.6 7.6 collective-permute-start
  268.8 7.6 collective-permute-start
  283.0 7.6 collective-permute-start
  297.2 7.6 collective-permute-start
  311.3 7.6 collective-permute-start
  326.1 7.6 collective-permute-start
  342.0 7.6 collective-permute-start
  358.9 7.6 collective-permute-start
  375.0 7.6 collective-permute-start
  390.2 7.6 collective-permute-start
  404.4 7.6 collective-permute-start
  418.6 7.6 collective-permute-start
  432.8 7.6 collective-permute-start
  447.0 7.6 collective-permute-start
  473.3 12.8 %all-reduce = (f32[2,512]{1,0:T(2,128)S(1)}, f32[2,512]{1,0:T(2,128)S(1)}) all-reduce(f32[2,512]{1,0:T(2,128)S(1)} %get-tuple-element.68, f32[2,512]{1,0:T(2,128)S(1)} %get-tuple-element.67), channel_id=1, replica_groups=mesh['seq'=32,'head'=8] {'head'}, use_global_device_ids=true, to_apply=%region_5.6 | all-reduce | flops 2048 | bytes 16384 | tf_op jit(solution)/shard_map/psum | solution.py:49
  494.9 382.0 %while.27 = (s32[]{:T(128)}, f32[4,128,128]{2,1,0:T(8,128)S(1)}, f32[4,128,128]{2,1,0:T(8,128)S(1)}, s32[]{:T(128)}, s32[]{:T(128)}) while((s32[]{:T(128)}, f32[4,128,128]{2,1,0:T(8,128)S(1)}, f32[4,128,128]{2,1,0:T(8,128)S(1)}, s32[]{:T(128)}, s32[]{:T(128)}) %tuple.55), condition=%wide.region_10.11_spmd.clone, body=%wide.region_9.10_spmd.clone.sunk | while | flops 131075 | bytes 2359407 | solution.py:64
  496.8 12.2 %collective-permute-done.1 = f32[4,128,128]{2,1,0:T(8,128)S(1)} collective-permute-done((f32[4,128,128]{2,1,0:T(8,128)S(1)}, f32[4,128,128]{2,1,0:T(8,128)S(1)}, u32[]{:S(2)}, u32[]{:S(2)}) %collective-permute-start.1) | collective-permute-done | bytes 262176 | tf_op jit(solution)/shard_map/while/body/eval_jaxpr/ppermute | solution.py:16
  511.0 11.0 %collective-permute-done.1 = f32[4,128,128]{2,1,0:T(8,128)S(1)} collective-permute-done((f32[4,128,128]{2,1,0:T(8,128)S(1)}, f32[4,128,128]{2,1,0:T(8,128)S(1)}, u32[]{:S(2)}, u32[]{:S(2)}) %collective-permute-start.1) | collective-permute-done | bytes 262176 | tf_op jit(solution)/shard_map/while/body/eval_jaxpr/ppermute | solution.py:16
  524.1 10.1 %collective-permute-done.1 = f32[4,128,128]{2,1,0:T(8,128)S(1)} collective-permute-done((f32[4,128,128]{2,1,0:T(8,128)S(1)}, f32[4,128,128]{2,1,0:T(8,128)S(1)}, u32[]{:S(2)}, u32[]{:S(2)}) %collective-permute-start.1) | collective-permute-done | bytes 262176 | tf_op jit(solution)/shard_map/while/body/eval_jaxpr/ppermute | solution.py:16
  536.2 9.7 %collective-permute-done.1 = f32[4,128,128]{2,1,0:T(8,128)S(1)} collective-permute-done((f32[4,128,128]{2,1,0:T(8,128)S(1)}, f32[4,128,128]{2,1,0:T(8,128)S(1)}, u32[]{:S(2)}, u32[]{:S(2)}) %collective-permute-start.1) | collective-permute-done | bytes 262176 | tf_op jit(solution)/shard_map/while/body/eval_jaxpr/ppermute | solution.py:16
  547.9 9.7 %collective-permute-done.1 = f32[4,128,128]{2,1,0:T(8,128)S(1)} collective-permute-done((f32[4,128,128]{2,1,0:T(8,128)S(1)}, f32[4,128,128]{2,1,0:T(8,128)S(1)}, u32[]{:S(2)}, u32[]{:S(2)}) %collective-permute-start.1) | collective-permute-done | bytes 262176 | tf_op jit(solution)/shard_map/while/body/eval_jaxpr/ppermute | solution.py:16
  559.6 9.7 %collective-permute-done.1 = f32[4,128,128]{2,1,0:T(8,128)S(1)} collective-permute-done((f32[4,128,128]{2,1,0:T(8,128)S(1)}, f32[4,128,128]{2,1,0:T(8,128)S(1)}, u32[]{:S(2)}, u32[]{:S(2)}) %collective-permute-start.1) | collective-permute-done | bytes 262176 | tf_op jit(solution)/shard_map/while/body/eval_jaxpr/ppermute | solution.py:16
  571.3 9.7 %collective-permute-done.1 = f32[4,128,128]{2,1,0:T(8,128)S(1)} collective-permute-done((f32[4,128,128]{2,1,0:T(8,128)S(1)}, f32[4,128,128]{2,1,0:T(8,128)S(1)}, u32[]{:S(2)}, u32[]{:S(2)}) %collective-permute-start.1) | collective-permute-done | bytes 262176 | tf_op jit(solution)/shard_map/while/body/eval_jaxpr/ppermute | solution.py:16
  583.0 9.8 %collective-permute-done.1 = f32[4,128,128]{2,1,0:T(8,128)S(1)} collective-permute-done((f32[4,128,128]{2,1,0:T(8,128)S(1)}, f32[4,128,128]{2,1,0:T(8,128)S(1)}, u32[]{:S(2)}, u32[]{:S(2)}) %collective-permute-start.1) | collective-permute-done | bytes 262176 | tf_op jit(solution)/shard_map/while/body/eval_jaxpr/ppermute | solution.py:16
  594.8 10.8 %collective-permute-done.1 = f32[4,128,128]{2,1,0:T(8,128)S(1)} collective-permute-done((f32[4,128,128]{2,1,0:T(8,128)S(1)}, f32[4,128,128]{2,1,0:T(8,128)S(1)}, u32[]{:S(2)}, u32[]{:S(2)}) %collective-permute-start.1) | collective-permute-done | bytes 262176 | tf_op jit(solution)/shard_map/while/body/eval_jaxpr/ppermute | solution.py:16
  607.7 12.1 %collective-permute-done.1 = f32[4,128,128]{2,1,0:T(8,128)S(1)} collective-permute-done((f32[4,128,128]{2,1,0:T(8,128)S(1)}, f32[4,128,128]{2,1,0:T(8,128)S(1)}, u32[]{:S(2)}, u32[]{:S(2)}) %collective-permute-start.1) | collective-permute-done | bytes 262176 | tf_op jit(solution)/shard_map/while/body/eval_jaxpr/ppermute | solution.py:16
  621.8 11.7 %collective-permute-done.1 = f32[4,128,128]{2,1,0:T(8,128)S(1)} collective-permute-done((f32[4,128,128]{2,1,0:T(8,128)S(1)}, f32[4,128,128]{2,1,0:T(8,128)S(1)}, u32[]{:S(2)}, u32[]{:S(2)}) %collective-permute-start.1) | collective-permute-done | bytes 262176 | tf_op jit(solution)/shard_map/while/body/eval_jaxpr/ppermute | solution.py:16
  635.6 10.9 %collective-permute-done.1 = f32[4,128,128]{2,1,0:T(8,128)S(1)} collective-permute-done((f32[4,128,128]{2,1,0:T(8,128)S(1)}, f32[4,128,128]{2,1,0:T(8,128)S(1)}, u32[]{:S(2)}, u32[]{:S(2)}) %collective-permute-start.1) | collective-permute-done | bytes 262176 | tf_op jit(solution)/shard_map/while/body/eval_jaxpr/ppermute | solution.py:16
  648.6 10.0 %collective-permute-done.1 = f32[4,128,128]{2,1,0:T(8,128)S(1)} collective-permute-done((f32[4,128,128]{2,1,0:T(8,128)S(1)}, f32[4,128,128]{2,1,0:T(8,128)S(1)}, u32[]{:S(2)}, u32[]{:S(2)}) %collective-permute-start.1) | collective-permute-done | bytes 262176 | tf_op jit(solution)/shard_map/while/body/eval_jaxpr/ppermute | solution.py:16
  660.6 9.7 %collective-permute-done.1 = f32[4,128,128]{2,1,0:T(8,128)S(1)} collective-permute-done((f32[4,128,128]{2,1,0:T(8,128)S(1)}, f32[4,128,128]{2,1,0:T(8,128)S(1)}, u32[]{:S(2)}, u32[]{:S(2)}) %collective-permute-start.1) | collective-permute-done | bytes 262176 | tf_op jit(solution)/shard_map/while/body/eval_jaxpr/ppermute | solution.py:16
  672.3 9.7 %collective-permute-done.1 = f32[4,128,128]{2,1,0:T(8,128)S(1)} collective-permute-done((f32[4,128,128]{2,1,0:T(8,128)S(1)}, f32[4,128,128]{2,1,0:T(8,128)S(1)}, u32[]{:S(2)}, u32[]{:S(2)}) %collective-permute-start.1) | collective-permute-done | bytes 262176 | tf_op jit(solution)/shard_map/while/body/eval_jaxpr/ppermute | solution.py:16
  684.0 9.7 %collective-permute-done.1 = f32[4,128,128]{2,1,0:T(8,128)S(1)} collective-permute-done((f32[4,128,128]{2,1,0:T(8,128)S(1)}, f32[4,128,128]{2,1,0:T(8,128)S(1)}, u32[]{:S(2)}, u32[]{:S(2)}) %collective-permute-start.1) | collective-permute-done | bytes 262176 | tf_op jit(solution)/shard_map/while/body/eval_jaxpr/ppermute | solution.py:16
  695.7 9.7 %collective-permute-done.1 = f32[4,128,128]{2,1,0:T(8,128)S(1)} collective-permute-done((f32[4,128,128]{2,1,0:T(8,128)S(1)}, f32[4,128,128]{2,1,0:T(8,128)S(1)}, u32[]{:S(2)}, u32[]{:S(2)}) %collective-permute-start.1) | collective-permute-done | bytes 262176 | tf_op jit(solution)/shard_map/while/body/eval_jaxpr/ppermute | solution.py:16
  707.4 9.8 %collective-permute-done.1 = f32[4,128,128]{2,1,0:T(8,128)S(1)} collective-permute-done((f32[4,128,128]{2,1,0:T(8,128)S(1)}, f32[4,128,128]{2,1,0:T(8,128)S(1)}, u32[]{:S(2)}, u32[]{:S(2)}) %collective-permute-start.1) | collective-permute-done | bytes 262176 | tf_op jit(solution)/shard_map/while/body/eval_jaxpr/ppermute | solution.py:16
  719.3 10.9 %collective-permute-done.1 = f32[4,128,128]{2,1,0:T(8,128)S(1)} collective-permute-done((f32[4,128,128]{2,1,0:T(8,128)S(1)}, f32[4,128,128]{2,1,0:T(8,128)S(1)}, u32[]{:S(2)}, u32[]{:S(2)}) %collective-permute-start.1) | collective-permute-done | bytes 262176 | tf_op jit(solution)/shard_map/while/body/eval_jaxpr/ppermute | solution.py:16
  732.3 12.2 %collective-permute-done.1 = f32[4,128,128]{2,1,0:T(8,128)S(1)} collective-permute-done((f32[4,128,128]{2,1,0:T(8,128)S(1)}, f32[4,128,128]{2,1,0:T(8,128)S(1)}, u32[]{:S(2)}, u32[]{:S(2)}) %collective-permute-start.1) | collective-permute-done | bytes 262176 | tf_op jit(solution)/shard_map/while/body/eval_jaxpr/ppermute | solution.py:16
  746.5 11.6 %collective-permute-done.1 = f32[4,128,128]{2,1,0:T(8,128)S(1)} collective-permute-done((f32[4,128,128]{2,1,0:T(8,128)S(1)}, f32[4,128,128]{2,1,0:T(8,128)S(1)}, u32[]{:S(2)}, u32[]{:S(2)}) %collective-permute-start.1) | collective-permute-done | bytes 262176 | tf_op jit(solution)/shard_map/while/body/eval_jaxpr/ppermute | solution.py:16
  760.2 10.8 %collective-permute-done.1 = f32[4,128,128]{2,1,0:T(8,128)S(1)} collective-permute-done((f32[4,128,128]{2,1,0:T(8,128)S(1)}, f32[4,128,128]{2,1,0:T(8,128)S(1)}, u32[]{:S(2)}, u32[]{:S(2)}) %collective-permute-start.1) | collective-permute-done | bytes 262176 | tf_op jit(solution)/shard_map/while/body/eval_jaxpr/ppermute | solution.py:16
  773.0 9.9 %collective-permute-done.1 = f32[4,128,128]{2,1,0:T(8,128)S(1)} collective-permute-done((f32[4,128,128]{2,1,0:T(8,128)S(1)}, f32[4,128,128]{2,1,0:T(8,128)S(1)}, u32[]{:S(2)}, u32[]{:S(2)}) %collective-permute-start.1) | collective-permute-done | bytes 262176 | tf_op jit(solution)/shard_map/while/body/eval_jaxpr/ppermute | solution.py:16
  784.9 9.7 %collective-permute-done.1 = f32[4,128,128]{2,1,0:T(8,128)S(1)} collective-permute-done((f32[4,128,128]{2,1,0:T(8,128)S(1)}, f32[4,128,128]{2,1,0:T(8,128)S(1)}, u32[]{:S(2)}, u32[]{:S(2)}) %collective-permute-start.1) | collective-permute-done | bytes 262176 | tf_op jit(solution)/shard_map/while/body/eval_jaxpr/ppermute | solution.py:16
  796.6 9.7 %collective-permute-done.1 = f32[4,128,128]{2,1,0:T(8,128)S(1)} collective-permute-done((f32[4,128,128]{2,1,0:T(8,128)S(1)}, f32[4,128,128]{2,1,0:T(8,128)S(1)}, u32[]{:S(2)}, u32[]{:S(2)}) %collective-permute-start.1) | collective-permute-done | bytes 262176 | tf_op jit(solution)/shard_map/while/body/eval_jaxpr/ppermute | solution.py:16
  808.3 9.7 %collective-permute-done.1 = f32[4,128,128]{2,1,0:T(8,128)S(1)} collective-permute-done((f32[4,128,128]{2,1,0:T(8,128)S(1)}, f32[4,128,128]{2,1,0:T(8,128)S(1)}, u32[]{:S(2)}, u32[]{:S(2)}) %collective-permute-start.1) | collective-permute-done | bytes 262176 | tf_op jit(solution)/shard_map/while/body/eval_jaxpr/ppermute | solution.py:16
  820.0 9.7 %collective-permute-done.1 = f32[4,128,128]{2,1,0:T(8,128)S(1)} collective-permute-done((f32[4,128,128]{2,1,0:T(8,128)S(1)}, f32[4,128,128]{2,1,0:T(8,128)S(1)}, u32[]{:S(2)}, u32[]{:S(2)}) %collective-permute-start.1) | collective-permute-done | bytes 262176 | tf_op jit(solution)/shard_map/while/body/eval_jaxpr/ppermute | solution.py:16
  831.8 10.0 %collective-permute-done.1 = f32[4,128,128]{2,1,0:T(8,128)S(1)} collective-permute-done((f32[4,128,128]{2,1,0:T(8,128)S(1)}, f32[4,128,128]{2,1,0:T(8,128)S(1)}, u32[]{:S(2)}, u32[]{:S(2)}) %collective-permute-start.1) | collective-permute-done | bytes 262176 | tf_op jit(solution)/shard_map/while/body/eval_jaxpr/ppermute | solution.py:16
  843.8 9.7 %collective-permute-done.1 = f32[4,128,128]{2,1,0:T(8,128)S(1)} collective-permute-done((f32[4,128,128]{2,1,0:T(8,128)S(1)}, f32[4,128,128]{2,1,0:T(8,128)S(1)}, u32[]{:S(2)}, u32[]{:S(2)}) %collective-permute-start.1) | collective-permute-done | bytes 262176 | tf_op jit(solution)/shard_map/while/body/eval_jaxpr/ppermute | solution.py:16
  855.5 9.7 %collective-permute-done.1 = f32[4,128,128]{2,1,0:T(8,128)S(1)} collective-permute-done((f32[4,128,128]{2,1,0:T(8,128)S(1)}, f32[4,128,128]{2,1,0:T(8,128)S(1)}, u32[]{:S(2)}, u32[]{:S(2)}) %collective-permute-start.1) | collective-permute-done | bytes 262176 | tf_op jit(solution)/shard_map/while/body/eval_jaxpr/ppermute | solution.py:16
  867.2 9.7 %collective-permute-done.1 = f32[4,128,128]{2,1,0:T(8,128)S(1)} collective-permute-done((f32[4,128,128]{2,1,0:T(8,128)S(1)}, f32[4,128,128]{2,1,0:T(8,128)S(1)}, u32[]{:S(2)}, u32[]{:S(2)}) %collective-permute-start.1) | collective-permute-done | bytes 262176 | tf_op jit(solution)/shard_map/while/body/eval_jaxpr/ppermute | solution.py:16
  (260 shorter events, 335.2 us)
Async XLA Ops:
  3.1 3.8 copy-start.7
  6.9 454.3 %copy-start.16 = (f32[2,4,128,128]{3,2,1,0:T(8,128)S(1)}, f32[2,4,128,128]{3,2,1,0:T(8,128)}, u32[]{:S(2)}) copy-start(f32[2,4,128,128]{3,2,1,0:T(8,128)} %get-tuple-element.88) | copy-start | bytes 1572868
  6.9 10.9 %collective-permute-start = (f32[4,128,128]{2,1,0:T(8,128)}, f32[4,128,128]{2,1,0:T(8,128)S(1)}, u32[]{:S(2)}, u32[]{:S(2)}) collective-permute-start(f32[4,128,128]{2,1,0:T(8,128)} %get-tuple-element.140), channel_id=1, source_target_pairs={{0,8},{8,16},{16,24},{24,32},{32,40},{40,48},{48,56},{56,64},{64,7... | collective-permute-start | bytes 786440 | tf_op jit(solution)/shard_map/while/body/eval_jaxpr/ppermute | solution.py:16
  19.3 12.6 %collective-permute-start = (f32[4,128,128]{2,1,0:T(8,128)}, f32[4,128,128]{2,1,0:T(8,128)S(1)}, u32[]{:S(2)}, u32[]{:S(2)}) collective-permute-start(f32[4,128,128]{2,1,0:T(8,128)} %get-tuple-element.140), channel_id=1, source_target_pairs={{0,8},{8,16},{16,24},{24,32},{32,40},{40,48},{48,56},{56,64},{64,7... | collective-permute-start | bytes 786440 | tf_op jit(solution)/shard_map/while/body/eval_jaxpr/ppermute | solution.py:16
  34.2 11.8 %collective-permute-start = (f32[4,128,128]{2,1,0:T(8,128)}, f32[4,128,128]{2,1,0:T(8,128)S(1)}, u32[]{:S(2)}, u32[]{:S(2)}) collective-permute-start(f32[4,128,128]{2,1,0:T(8,128)} %get-tuple-element.140), channel_id=1, source_target_pairs={{0,8},{8,16},{16,24},{24,32},{32,40},{40,48},{48,56},{56,64},{64,7... | collective-permute-start | bytes 786440 | tf_op jit(solution)/shard_map/while/body/eval_jaxpr/ppermute | solution.py:16
  48.4 11.8 %collective-permute-start = (f32[4,128,128]{2,1,0:T(8,128)}, f32[4,128,128]{2,1,0:T(8,128)S(1)}, u32[]{:S(2)}, u32[]{:S(2)}) collective-permute-start(f32[4,128,128]{2,1,0:T(8,128)} %get-tuple-element.140), channel_id=1, source_target_pairs={{0,8},{8,16},{16,24},{24,32},{32,40},{40,48},{48,56},{56,64},{64,7... | collective-permute-start | bytes 786440 | tf_op jit(solution)/shard_map/while/body/eval_jaxpr/ppermute | solution.py:16
  62.6 11.8 %collective-permute-start = (f32[4,128,128]{2,1,0:T(8,128)}, f32[4,128,128]{2,1,0:T(8,128)S(1)}, u32[]{:S(2)}, u32[]{:S(2)}) collective-permute-start(f32[4,128,128]{2,1,0:T(8,128)} %get-tuple-element.140), channel_id=1, source_target_pairs={{0,8},{8,16},{16,24},{24,32},{32,40},{40,48},{48,56},{56,64},{64,7... | collective-permute-start | bytes 786440 | tf_op jit(solution)/shard_map/while/body/eval_jaxpr/ppermute | solution.py:16
  76.7 11.8 %collective-permute-start = (f32[4,128,128]{2,1,0:T(8,128)}, f32[4,128,128]{2,1,0:T(8,128)S(1)}, u32[]{:S(2)}, u32[]{:S(2)}) collective-permute-start(f32[4,128,128]{2,1,0:T(8,128)} %get-tuple-element.140), channel_id=1, source_target_pairs={{0,8},{8,16},{16,24},{24,32},{32,40},{40,48},{48,56},{56,64},{64,7... | collective-permute-start | bytes 786440 | tf_op jit(solution)/shard_map/while/body/eval_jaxpr/ppermute | solution.py:16
  90.9 11.8 %collective-permute-start = (f32[4,128,128]{2,1,0:T(8,128)}, f32[4,128,128]{2,1,0:T(8,128)S(1)}, u32[]{:S(2)}, u32[]{:S(2)}) collective-permute-start(f32[4,128,128]{2,1,0:T(8,128)} %get-tuple-element.140), channel_id=1, source_target_pairs={{0,8},{8,16},{16,24},{24,32},{32,40},{40,48},{48,56},{56,64},{64,7... | collective-permute-start | bytes 786440 | tf_op jit(solution)/shard_map/while/body/eval_jaxpr/ppermute | solution.py:16
  105.1 11.8 %collective-permute-start = (f32[4,128,128]{2,1,0:T(8,128)}, f32[4,128,128]{2,1,0:T(8,128)S(1)}, u32[]{:S(2)}, u32[]{:S(2)}) collective-permute-start(f32[4,128,128]{2,1,0:T(8,128)} %get-tuple-element.140), channel_id=1, source_target_pairs={{0,8},{8,16},{16,24},{24,32},{32,40},{40,48},{48,56},{56,64},{64,7... | collective-permute-start | bytes 786440 | tf_op jit(solution)/shard_map/while/body/eval_jaxpr/ppermute | solution.py:16
  119.3 11.8 %collective-permute-start = (f32[4,128,128]{2,1,0:T(8,128)}, f32[4,128,128]{2,1,0:T(8,128)S(1)}, u32[]{:S(2)}, u32[]{:S(2)}) collective-permute-start(f32[4,128,128]{2,1,0:T(8,128)} %get-tuple-element.140), channel_id=1, source_target_pairs={{0,8},{8,16},{16,24},{24,32},{32,40},{40,48},{48,56},{56,64},{64,7... | collective-permute-start | bytes 786440 | tf_op jit(solution)/shard_map/while/body/eval_jaxpr/ppermute | solution.py:16
  133.4 12.5 %collective-permute-start = (f32[4,128,128]{2,1,0:T(8,128)}, f32[4,128,128]{2,1,0:T(8,128)S(1)}, u32[]{:S(2)}, u32[]{:S(2)}) collective-permute-start(f32[4,128,128]{2,1,0:T(8,128)} %get-tuple-element.140), channel_id=1, source_target_pairs={{0,8},{8,16},{16,24},{24,32},{32,40},{40,48},{48,56},{56,64},{64,7... | collective-permute-start | bytes 786440 | tf_op jit(solution)/shard_map/while/body/eval_jaxpr/ppermute | solution.py:16
  148.3 13.6 %collective-permute-start = (f32[4,128,128]{2,1,0:T(8,128)}, f32[4,128,128]{2,1,0:T(8,128)S(1)}, u32[]{:S(2)}, u32[]{:S(2)}) collective-permute-start(f32[4,128,128]{2,1,0:T(8,128)} %get-tuple-element.140), channel_id=1, source_target_pairs={{0,8},{8,16},{16,24},{24,32},{32,40},{40,48},{48,56},{56,64},{64,7... | collective-permute-start | bytes 786440 | tf_op jit(solution)/shard_map/while/body/eval_jaxpr/ppermute | solution.py:16
  164.3 14.4 %collective-permute-start = (f32[4,128,128]{2,1,0:T(8,128)}, f32[4,128,128]{2,1,0:T(8,128)S(1)}, u32[]{:S(2)}, u32[]{:S(2)}) collective-permute-start(f32[4,128,128]{2,1,0:T(8,128)} %get-tuple-element.140), channel_id=1, source_target_pairs={{0,8},{8,16},{16,24},{24,32},{32,40},{40,48},{48,56},{56,64},{64,7... | collective-permute-start | bytes 786440 | tf_op jit(solution)/shard_map/while/body/eval_jaxpr/ppermute | solution.py:16
  181.1 13.5 %collective-permute-start = (f32[4,128,128]{2,1,0:T(8,128)}, f32[4,128,128]{2,1,0:T(8,128)S(1)}, u32[]{:S(2)}, u32[]{:S(2)}) collective-permute-start(f32[4,128,128]{2,1,0:T(8,128)} %get-tuple-element.140), channel_id=1, source_target_pairs={{0,8},{8,16},{16,24},{24,32},{32,40},{40,48},{48,56},{56,64},{64,7... | collective-permute-start | bytes 786440 | tf_op jit(solution)/shard_map/while/body/eval_jaxpr/ppermute | solution.py:16
  197.0 12.7 %collective-permute-start = (f32[4,128,128]{2,1,0:T(8,128)}, f32[4,128,128]{2,1,0:T(8,128)S(1)}, u32[]{:S(2)}, u32[]{:S(2)}) collective-permute-start(f32[4,128,128]{2,1,0:T(8,128)} %get-tuple-element.140), channel_id=1, source_target_pairs={{0,8},{8,16},{16,24},{24,32},{32,40},{40,48},{48,56},{56,64},{64,7... | collective-permute-start | bytes 786440 | tf_op jit(solution)/shard_map/while/body/eval_jaxpr/ppermute | solution.py:16
  212.1 11.8 %collective-permute-start = (f32[4,128,128]{2,1,0:T(8,128)}, f32[4,128,128]{2,1,0:T(8,128)S(1)}, u32[]{:S(2)}, u32[]{:S(2)}) collective-permute-start(f32[4,128,128]{2,1,0:T(8,128)} %get-tuple-element.140), channel_id=1, source_target_pairs={{0,8},{8,16},{16,24},{24,32},{32,40},{40,48},{48,56},{56,64},{64,7... | collective-permute-start | bytes 786440 | tf_op jit(solution)/shard_map/while/body/eval_jaxpr/ppermute | solution.py:16
  226.3 11.8 %collective-permute-start = (f32[4,128,128]{2,1,0:T(8,128)}, f32[4,128,128]{2,1,0:T(8,128)S(1)}, u32[]{:S(2)}, u32[]{:S(2)}) collective-permute-start(f32[4,128,128]{2,1,0:T(8,128)} %get-tuple-element.140), channel_id=1, source_target_pairs={{0,8},{8,16},{16,24},{24,32},{32,40},{40,48},{48,56},{56,64},{64,7... | collective-permute-start | bytes 786440 | tf_op jit(solution)/shard_map/while/body/eval_jaxpr/ppermute | solution.py:16
  240.5 11.8 %collective-permute-start = (f32[4,128,128]{2,1,0:T(8,128)}, f32[4,128,128]{2,1,0:T(8,128)S(1)}, u32[]{:S(2)}, u32[]{:S(2)}) collective-permute-start(f32[4,128,128]{2,1,0:T(8,128)} %get-tuple-element.140), channel_id=1, source_target_pairs={{0,8},{8,16},{16,24},{24,32},{32,40},{40,48},{48,56},{56,64},{64,7... | collective-permute-start | bytes 786440 | tf_op jit(solution)/shard_map/while/body/eval_jaxpr/ppermute | solution.py:16
  254.6 11.8 %collective-permute-start = (f32[4,128,128]{2,1,0:T(8,128)}, f32[4,128,128]{2,1,0:T(8,128)S(1)}, u32[]{:S(2)}, u32[]{:S(2)}) collective-permute-start(f32[4,128,128]{2,1,0:T(8,128)} %get-tuple-element.140), channel_id=1, source_target_pairs={{0,8},{8,16},{16,24},{24,32},{32,40},{40,48},{48,56},{56,64},{64,7... | collective-permute-start | bytes 786440 | tf_op jit(solution)/shard_map/while/body/eval_jaxpr/ppermute | solution.py:16
  268.8 11.8 %collective-permute-start = (f32[4,128,128]{2,1,0:T(8,128)}, f32[4,128,128]{2,1,0:T(8,128)S(1)}, u32[]{:S(2)}, u32[]{:S(2)}) collective-permute-start(f32[4,128,128]{2,1,0:T(8,128)} %get-tuple-element.140), channel_id=1, source_target_pairs={{0,8},{8,16},{16,24},{24,32},{32,40},{40,48},{48,56},{56,64},{64,7... | collective-permute-start | bytes 786440 | tf_op jit(solution)/shard_map/while/body/eval_jaxpr/ppermute | solution.py:16
  283.0 11.8 %collective-permute-start = (f32[4,128,128]{2,1,0:T(8,128)}, f32[4,128,128]{2,1,0:T(8,128)S(1)}, u32[]{:S(2)}, u32[]{:S(2)}) collective-permute-start(f32[4,128,128]{2,1,0:T(8,128)} %get-tuple-element.140), channel_id=1, source_target_pairs={{0,8},{8,16},{16,24},{24,32},{32,40},{40,48},{48,56},{56,64},{64,7... | collective-permute-start | bytes 786440 | tf_op jit(solution)/shard_map/while/body/eval_jaxpr/ppermute | solution.py:16
  297.2 11.8 %collective-permute-start = (f32[4,128,128]{2,1,0:T(8,128)}, f32[4,128,128]{2,1,0:T(8,128)S(1)}, u32[]{:S(2)}, u32[]{:S(2)}) collective-permute-start(f32[4,128,128]{2,1,0:T(8,128)} %get-tuple-element.140), channel_id=1, source_target_pairs={{0,8},{8,16},{16,24},{24,32},{32,40},{40,48},{48,56},{56,64},{64,7... | collective-permute-start | bytes 786440 | tf_op jit(solution)/shard_map/while/body/eval_jaxpr/ppermute | solution.py:16
  311.3 12.4 %collective-permute-start = (f32[4,128,128]{2,1,0:T(8,128)}, f32[4,128,128]{2,1,0:T(8,128)S(1)}, u32[]{:S(2)}, u32[]{:S(2)}) collective-permute-start(f32[4,128,128]{2,1,0:T(8,128)} %get-tuple-element.140), channel_id=1, source_target_pairs={{0,8},{8,16},{16,24},{24,32},{32,40},{40,48},{48,56},{56,64},{64,7... | collective-permute-start | bytes 786440 | tf_op jit(solution)/shard_map/while/body/eval_jaxpr/ppermute | solution.py:16
  326.1 13.5 %collective-permute-start = (f32[4,128,128]{2,1,0:T(8,128)}, f32[4,128,128]{2,1,0:T(8,128)S(1)}, u32[]{:S(2)}, u32[]{:S(2)}) collective-permute-start(f32[4,128,128]{2,1,0:T(8,128)} %get-tuple-element.140), channel_id=1, source_target_pairs={{0,8},{8,16},{16,24},{24,32},{32,40},{40,48},{48,56},{56,64},{64,7... | collective-permute-start | bytes 786440 | tf_op jit(solution)/shard_map/while/body/eval_jaxpr/ppermute | solution.py:16
  342.0 14.5 %collective-permute-start = (f32[4,128,128]{2,1,0:T(8,128)}, f32[4,128,128]{2,1,0:T(8,128)S(1)}, u32[]{:S(2)}, u32[]{:S(2)}) collective-permute-start(f32[4,128,128]{2,1,0:T(8,128)} %get-tuple-element.140), channel_id=1, source_target_pairs={{0,8},{8,16},{16,24},{24,32},{32,40},{40,48},{48,56},{56,64},{64,7... | collective-permute-start | bytes 786440 | tf_op jit(solution)/shard_map/while/body/eval_jaxpr/ppermute | solution.py:16
  358.9 13.7 %collective-permute-start = (f32[4,128,128]{2,1,0:T(8,128)}, f32[4,128,128]{2,1,0:T(8,128)S(1)}, u32[]{:S(2)}, u32[]{:S(2)}) collective-permute-start(f32[4,128,128]{2,1,0:T(8,128)} %get-tuple-element.140), channel_id=1, source_target_pairs={{0,8},{8,16},{16,24},{24,32},{32,40},{40,48},{48,56},{56,64},{64,7... | collective-permute-start | bytes 786440 | tf_op jit(solution)/shard_map/while/body/eval_jaxpr/ppermute | solution.py:16
  375.0 12.8 %collective-permute-start = (f32[4,128,128]{2,1,0:T(8,128)}, f32[4,128,128]{2,1,0:T(8,128)S(1)}, u32[]{:S(2)}, u32[]{:S(2)}) collective-permute-start(f32[4,128,128]{2,1,0:T(8,128)} %get-tuple-element.140), channel_id=1, source_target_pairs={{0,8},{8,16},{16,24},{24,32},{32,40},{40,48},{48,56},{56,64},{64,7... | collective-permute-start | bytes 786440 | tf_op jit(solution)/shard_map/while/body/eval_jaxpr/ppermute | solution.py:16
  390.2 11.9 %collective-permute-start = (f32[4,128,128]{2,1,0:T(8,128)}, f32[4,128,128]{2,1,0:T(8,128)S(1)}, u32[]{:S(2)}, u32[]{:S(2)}) collective-permute-start(f32[4,128,128]{2,1,0:T(8,128)} %get-tuple-element.140), channel_id=1, source_target_pairs={{0,8},{8,16},{16,24},{24,32},{32,40},{40,48},{48,56},{56,64},{64,7... | collective-permute-start | bytes 786440 | tf_op jit(solution)/shard_map/while/body/eval_jaxpr/ppermute | solution.py:16
  404.4 11.8 %collective-permute-start = (f32[4,128,128]{2,1,0:T(8,128)}, f32[4,128,128]{2,1,0:T(8,128)S(1)}, u32[]{:S(2)}, u32[]{:S(2)}) collective-permute-start(f32[4,128,128]{2,1,0:T(8,128)} %get-tuple-element.140), channel_id=1, source_target_pairs={{0,8},{8,16},{16,24},{24,32},{32,40},{40,48},{48,56},{56,64},{64,7... | collective-permute-start | bytes 786440 | tf_op jit(solution)/shard_map/while/body/eval_jaxpr/ppermute | solution.py:16
  418.6 11.8 %collective-permute-start = (f32[4,128,128]{2,1,0:T(8,128)}, f32[4,128,128]{2,1,0:T(8,128)S(1)}, u32[]{:S(2)}, u32[]{:S(2)}) collective-permute-start(f32[4,128,128]{2,1,0:T(8,128)} %get-tuple-element.140), channel_id=1, source_target_pairs={{0,8},{8,16},{16,24},{24,32},{32,40},{40,48},{48,56},{56,64},{64,7... | collective-permute-start | bytes 786440 | tf_op jit(solution)/shard_map/while/body/eval_jaxpr/ppermute | solution.py:16
  432.8 11.8 %collective-permute-start = (f32[4,128,128]{2,1,0:T(8,128)}, f32[4,128,128]{2,1,0:T(8,128)S(1)}, u32[]{:S(2)}, u32[]{:S(2)}) collective-permute-start(f32[4,128,128]{2,1,0:T(8,128)} %get-tuple-element.140), channel_id=1, source_target_pairs={{0,8},{8,16},{16,24},{24,32},{32,40},{40,48},{48,56},{56,64},{64,7... | collective-permute-start | bytes 786440 | tf_op jit(solution)/shard_map/while/body/eval_jaxpr/ppermute | solution.py:16
  447.0 11.8 %collective-permute-start = (f32[4,128,128]{2,1,0:T(8,128)}, f32[4,128,128]{2,1,0:T(8,128)S(1)}, u32[]{:S(2)}, u32[]{:S(2)}) collective-permute-start(f32[4,128,128]{2,1,0:T(8,128)} %get-tuple-element.140), channel_id=1, source_target_pairs={{0,8},{8,16},{16,24},{24,32},{32,40},{40,48},{48,56},{56,64},{64,7... | collective-permute-start | bytes 786440 | tf_op jit(solution)/shard_map/while/body/eval_jaxpr/ppermute | solution.py:16
  494.9 14.1 %collective-permute-start.1 = (f32[4,128,128]{2,1,0:T(8,128)S(1)}, f32[4,128,128]{2,1,0:T(8,128)S(1)}, u32[]{:S(2)}, u32[]{:S(2)}) collective-permute-start(f32[4,128,128]{2,1,0:T(8,128)S(1)} %get-tuple-element.155), channel_id=1, source_target_pairs={{8,0},{16,8},{24,16},{32,24},{40,32},{48,40},{56,48},{64,56},{72,6... | collective-permute-start | bytes 786440 | tf_op jit(solution)/shard_map/while/body/eval_jaxpr/ppermute | solution.py:16
  509.1 12.9 %collective-permute-start.1 = (f32[4,128,128]{2,1,0:T(8,128)S(1)}, f32[4,128,128]{2,1,0:T(8,128)S(1)}, u32[]{:S(2)}, u32[]{:S(2)}) collective-permute-start(f32[4,128,128]{2,1,0:T(8,128)S(1)} %get-tuple-element.155), channel_id=1, source_target_pairs={{8,0},{16,8},{24,16},{32,24},{40,32},{48,40},{56,48},{64,56},{72,6... | collective-permute-start | bytes 786440 | tf_op jit(solution)/shard_map/while/body/eval_jaxpr/ppermute | solution.py:16
  522.1 12.0 %collective-permute-start.1 = (f32[4,128,128]{2,1,0:T(8,128)S(1)}, f32[4,128,128]{2,1,0:T(8,128)S(1)}, u32[]{:S(2)}, u32[]{:S(2)}) collective-permute-start(f32[4,128,128]{2,1,0:T(8,128)S(1)} %get-tuple-element.155), channel_id=1, source_target_pairs={{8,0},{16,8},{24,16},{32,24},{40,32},{48,40},{56,48},{64,56},{72,6... | collective-permute-start | bytes 786440 | tf_op jit(solution)/shard_map/while/body/eval_jaxpr/ppermute | solution.py:16
  534.2 11.6 %collective-permute-start.1 = (f32[4,128,128]{2,1,0:T(8,128)S(1)}, f32[4,128,128]{2,1,0:T(8,128)S(1)}, u32[]{:S(2)}, u32[]{:S(2)}) collective-permute-start(f32[4,128,128]{2,1,0:T(8,128)S(1)} %get-tuple-element.155), channel_id=1, source_target_pairs={{8,0},{16,8},{24,16},{32,24},{40,32},{48,40},{56,48},{64,56},{72,6... | collective-permute-start | bytes 786440 | tf_op jit(solution)/shard_map/while/body/eval_jaxpr/ppermute | solution.py:16
  546.0 11.6 %collective-permute-start.1 = (f32[4,128,128]{2,1,0:T(8,128)S(1)}, f32[4,128,128]{2,1,0:T(8,128)S(1)}, u32[]{:S(2)}, u32[]{:S(2)}) collective-permute-start(f32[4,128,128]{2,1,0:T(8,128)S(1)} %get-tuple-element.155), channel_id=1, source_target_pairs={{8,0},{16,8},{24,16},{32,24},{40,32},{48,40},{56,48},{64,56},{72,6... | collective-permute-start | bytes 786440 | tf_op jit(solution)/shard_map/while/body/eval_jaxpr/ppermute | solution.py:16
  557.7 11.6 %collective-permute-start.1 = (f32[4,128,128]{2,1,0:T(8,128)S(1)}, f32[4,128,128]{2,1,0:T(8,128)S(1)}, u32[]{:S(2)}, u32[]{:S(2)}) collective-permute-start(f32[4,128,128]{2,1,0:T(8,128)S(1)} %get-tuple-element.155), channel_id=1, source_target_pairs={{8,0},{16,8},{24,16},{32,24},{40,32},{48,40},{56,48},{64,56},{72,6... | collective-permute-start | bytes 786440 | tf_op jit(solution)/shard_map/while/body/eval_jaxpr/ppermute | solution.py:16
  569.4 11.6 %collective-permute-start.1 = (f32[4,128,128]{2,1,0:T(8,128)S(1)}, f32[4,128,128]{2,1,0:T(8,128)S(1)}, u32[]{:S(2)}, u32[]{:S(2)}) collective-permute-start(f32[4,128,128]{2,1,0:T(8,128)S(1)} %get-tuple-element.155), channel_id=1, source_target_pairs={{8,0},{16,8},{24,16},{32,24},{40,32},{48,40},{56,48},{64,56},{72,6... | collective-permute-start | bytes 786440 | tf_op jit(solution)/shard_map/while/body/eval_jaxpr/ppermute | solution.py:16
  581.1 11.7 %collective-permute-start.1 = (f32[4,128,128]{2,1,0:T(8,128)S(1)}, f32[4,128,128]{2,1,0:T(8,128)S(1)}, u32[]{:S(2)}, u32[]{:S(2)}) collective-permute-start(f32[4,128,128]{2,1,0:T(8,128)S(1)} %get-tuple-element.155), channel_id=1, source_target_pairs={{8,0},{16,8},{24,16},{32,24},{40,32},{48,40},{56,48},{64,56},{72,6... | collective-permute-start | bytes 786440 | tf_op jit(solution)/shard_map/while/body/eval_jaxpr/ppermute | solution.py:16
  592.9 12.8 %collective-permute-start.1 = (f32[4,128,128]{2,1,0:T(8,128)S(1)}, f32[4,128,128]{2,1,0:T(8,128)S(1)}, u32[]{:S(2)}, u32[]{:S(2)}) collective-permute-start(f32[4,128,128]{2,1,0:T(8,128)S(1)} %get-tuple-element.155), channel_id=1, source_target_pairs={{8,0},{16,8},{24,16},{32,24},{40,32},{48,40},{56,48},{64,56},{72,6... | collective-permute-start | bytes 786440 | tf_op jit(solution)/shard_map/while/body/eval_jaxpr/ppermute | solution.py:16
  605.8 14.0 %collective-permute-start.1 = (f32[4,128,128]{2,1,0:T(8,128)S(1)}, f32[4,128,128]{2,1,0:T(8,128)S(1)}, u32[]{:S(2)}, u32[]{:S(2)}) collective-permute-start(f32[4,128,128]{2,1,0:T(8,128)S(1)} %get-tuple-element.155), channel_id=1, source_target_pairs={{8,0},{16,8},{24,16},{32,24},{40,32},{48,40},{56,48},{64,56},{72,6... | collective-permute-start | bytes 786440 | tf_op jit(solution)/shard_map/while/body/eval_jaxpr/ppermute | solution.py:16
  619.9 13.6 %collective-permute-start.1 = (f32[4,128,128]{2,1,0:T(8,128)S(1)}, f32[4,128,128]{2,1,0:T(8,128)S(1)}, u32[]{:S(2)}, u32[]{:S(2)}) collective-permute-start(f32[4,128,128]{2,1,0:T(8,128)S(1)} %get-tuple-element.155), channel_id=1, source_target_pairs={{8,0},{16,8},{24,16},{32,24},{40,32},{48,40},{56,48},{64,56},{72,6... | collective-permute-start | bytes 786440 | tf_op jit(solution)/shard_map/while/body/eval_jaxpr/ppermute | solution.py:16
  633.7 12.8 %collective-permute-start.1 = (f32[4,128,128]{2,1,0:T(8,128)S(1)}, f32[4,128,128]{2,1,0:T(8,128)S(1)}, u32[]{:S(2)}, u32[]{:S(2)}) collective-permute-start(f32[4,128,128]{2,1,0:T(8,128)S(1)} %get-tuple-element.155), channel_id=1, source_target_pairs={{8,0},{16,8},{24,16},{32,24},{40,32},{48,40},{56,48},{64,56},{72,6... | collective-permute-start | bytes 786440 | tf_op jit(solution)/shard_map/while/body/eval_jaxpr/ppermute | solution.py:16
  646.6 11.9 %collective-permute-start.1 = (f32[4,128,128]{2,1,0:T(8,128)S(1)}, f32[4,128,128]{2,1,0:T(8,128)S(1)}, u32[]{:S(2)}, u32[]{:S(2)}) collective-permute-start(f32[4,128,128]{2,1,0:T(8,128)S(1)} %get-tuple-element.155), channel_id=1, source_target_pairs={{8,0},{16,8},{24,16},{32,24},{40,32},{48,40},{56,48},{64,56},{72,6... | collective-permute-start | bytes 786440 | tf_op jit(solution)/shard_map/while/body/eval_jaxpr/ppermute | solution.py:16
  658.6 11.6 %collective-permute-start.1 = (f32[4,128,128]{2,1,0:T(8,128)S(1)}, f32[4,128,128]{2,1,0:T(8,128)S(1)}, u32[]{:S(2)}, u32[]{:S(2)}) collective-permute-start(f32[4,128,128]{2,1,0:T(8,128)S(1)} %get-tuple-element.155), channel_id=1, source_target_pairs={{8,0},{16,8},{24,16},{32,24},{40,32},{48,40},{56,48},{64,56},{72,6... | collective-permute-start | bytes 786440 | tf_op jit(solution)/shard_map/while/body/eval_jaxpr/ppermute | solution.py:16
  670.3 11.6 %collective-permute-start.1 = (f32[4,128,128]{2,1,0:T(8,128)S(1)}, f32[4,128,128]{2,1,0:T(8,128)S(1)}, u32[]{:S(2)}, u32[]{:S(2)}) collective-permute-start(f32[4,128,128]{2,1,0:T(8,128)S(1)} %get-tuple-element.155), channel_id=1, source_target_pairs={{8,0},{16,8},{24,16},{32,24},{40,32},{48,40},{56,48},{64,56},{72,6... | collective-permute-start | bytes 786440 | tf_op jit(solution)/shard_map/while/body/eval_jaxpr/ppermute | solution.py:16
  682.1 11.6 %collective-permute-start.1 = (f32[4,128,128]{2,1,0:T(8,128)S(1)}, f32[4,128,128]{2,1,0:T(8,128)S(1)}, u32[]{:S(2)}, u32[]{:S(2)}) collective-permute-start(f32[4,128,128]{2,1,0:T(8,128)S(1)} %get-tuple-element.155), channel_id=1, source_target_pairs={{8,0},{16,8},{24,16},{32,24},{40,32},{48,40},{56,48},{64,56},{72,6... | collective-permute-start | bytes 786440 | tf_op jit(solution)/shard_map/while/body/eval_jaxpr/ppermute | solution.py:16
  693.8 11.6 %collective-permute-start.1 = (f32[4,128,128]{2,1,0:T(8,128)S(1)}, f32[4,128,128]{2,1,0:T(8,128)S(1)}, u32[]{:S(2)}, u32[]{:S(2)}) collective-permute-start(f32[4,128,128]{2,1,0:T(8,128)S(1)} %get-tuple-element.155), channel_id=1, source_target_pairs={{8,0},{16,8},{24,16},{32,24},{40,32},{48,40},{56,48},{64,56},{72,6... | collective-permute-start | bytes 786440 | tf_op jit(solution)/shard_map/while/body/eval_jaxpr/ppermute | solution.py:16
  705.5 11.8 %collective-permute-start.1 = (f32[4,128,128]{2,1,0:T(8,128)S(1)}, f32[4,128,128]{2,1,0:T(8,128)S(1)}, u32[]{:S(2)}, u32[]{:S(2)}) collective-permute-start(f32[4,128,128]{2,1,0:T(8,128)S(1)} %get-tuple-element.155), channel_id=1, source_target_pairs={{8,0},{16,8},{24,16},{32,24},{40,32},{48,40},{56,48},{64,56},{72,6... | collective-permute-start | bytes 786440 | tf_op jit(solution)/shard_map/while/body/eval_jaxpr/ppermute | solution.py:16
  717.4 12.9 %collective-permute-start.1 = (f32[4,128,128]{2,1,0:T(8,128)S(1)}, f32[4,128,128]{2,1,0:T(8,128)S(1)}, u32[]{:S(2)}, u32[]{:S(2)}) collective-permute-start(f32[4,128,128]{2,1,0:T(8,128)S(1)} %get-tuple-element.155), channel_id=1, source_target_pairs={{8,0},{16,8},{24,16},{32,24},{40,32},{48,40},{56,48},{64,56},{72,6... | collective-permute-start | bytes 786440 | tf_op jit(solution)/shard_map/while/body/eval_jaxpr/ppermute | solution.py:16
  730.4 14.1 %collective-permute-start.1 = (f32[4,128,128]{2,1,0:T(8,128)S(1)}, f32[4,128,128]{2,1,0:T(8,128)S(1)}, u32[]{:S(2)}, u32[]{:S(2)}) collective-permute-start(f32[4,128,128]{2,1,0:T(8,128)S(1)} %get-tuple-element.155), channel_id=1, source_target_pairs={{8,0},{16,8},{24,16},{32,24},{40,32},{48,40},{56,48},{64,56},{72,6... | collective-permute-start | bytes 786440 | tf_op jit(solution)/shard_map/while/body/eval_jaxpr/ppermute | solution.py:16
  744.6 13.5 %collective-permute-start.1 = (f32[4,128,128]{2,1,0:T(8,128)S(1)}, f32[4,128,128]{2,1,0:T(8,128)S(1)}, u32[]{:S(2)}, u32[]{:S(2)}) collective-permute-start(f32[4,128,128]{2,1,0:T(8,128)S(1)} %get-tuple-element.155), channel_id=1, source_target_pairs={{8,0},{16,8},{24,16},{32,24},{40,32},{48,40},{56,48},{64,56},{72,6... | collective-permute-start | bytes 786440 | tf_op jit(solution)/shard_map/while/body/eval_jaxpr/ppermute | solution.py:16
  758.3 12.7 %collective-permute-start.1 = (f32[4,128,128]{2,1,0:T(8,128)S(1)}, f32[4,128,128]{2,1,0:T(8,128)S(1)}, u32[]{:S(2)}, u32[]{:S(2)}) collective-permute-start(f32[4,128,128]{2,1,0:T(8,128)S(1)} %get-tuple-element.155), channel_id=1, source_target_pairs={{8,0},{16,8},{24,16},{32,24},{40,32},{48,40},{56,48},{64,56},{72,6... | collective-permute-start | bytes 786440 | tf_op jit(solution)/shard_map/while/body/eval_jaxpr/ppermute | solution.py:16
  771.1 11.8 %collective-permute-start.1 = (f32[4,128,128]{2,1,0:T(8,128)S(1)}, f32[4,128,128]{2,1,0:T(8,128)S(1)}, u32[]{:S(2)}, u32[]{:S(2)}) collective-permute-start(f32[4,128,128]{2,1,0:T(8,128)S(1)} %get-tuple-element.155), channel_id=1, source_target_pairs={{8,0},{16,8},{24,16},{32,24},{40,32},{48,40},{56,48},{64,56},{72,6... | collective-permute-start | bytes 786440 | tf_op jit(solution)/shard_map/while/body/eval_jaxpr/ppermute | solution.py:16
  783.0 11.6 %collective-permute-start.1 = (f32[4,128,128]{2,1,0:T(8,128)S(1)}, f32[4,128,128]{2,1,0:T(8,128)S(1)}, u32[]{:S(2)}, u32[]{:S(2)}) collective-permute-start(f32[4,128,128]{2,1,0:T(8,128)S(1)} %get-tuple-element.155), channel_id=1, source_target_pairs={{8,0},{16,8},{24,16},{32,24},{40,32},{48,40},{56,48},{64,56},{72,6... | collective-permute-start | bytes 786440 | tf_op jit(solution)/shard_map/while/body/eval_jaxpr/ppermute | solution.py:16
  794.7 11.6 %collective-permute-start.1 = (f32[4,128,128]{2,1,0:T(8,128)S(1)}, f32[4,128,128]{2,1,0:T(8,128)S(1)}, u32[]{:S(2)}, u32[]{:S(2)}) collective-permute-start(f32[4,128,128]{2,1,0:T(8,128)S(1)} %get-tuple-element.155), channel_id=1, source_target_pairs={{8,0},{16,8},{24,16},{32,24},{40,32},{48,40},{56,48},{64,56},{72,6... | collective-permute-start | bytes 786440 | tf_op jit(solution)/shard_map/while/body/eval_jaxpr/ppermute | solution.py:16
  806.4 11.6 %collective-permute-start.1 = (f32[4,128,128]{2,1,0:T(8,128)S(1)}, f32[4,128,128]{2,1,0:T(8,128)S(1)}, u32[]{:S(2)}, u32[]{:S(2)}) collective-permute-start(f32[4,128,128]{2,1,0:T(8,128)S(1)} %get-tuple-element.155), channel_id=1, source_target_pairs={{8,0},{16,8},{24,16},{32,24},{40,32},{48,40},{56,48},{64,56},{72,6... | collective-permute-start | bytes 786440 | tf_op jit(solution)/shard_map/while/body/eval_jaxpr/ppermute | solution.py:16
  818.1 11.6 %collective-permute-start.1 = (f32[4,128,128]{2,1,0:T(8,128)S(1)}, f32[4,128,128]{2,1,0:T(8,128)S(1)}, u32[]{:S(2)}, u32[]{:S(2)}) collective-permute-start(f32[4,128,128]{2,1,0:T(8,128)S(1)} %get-tuple-element.155), channel_id=1, source_target_pairs={{8,0},{16,8},{24,16},{32,24},{40,32},{48,40},{56,48},{64,56},{72,6... | collective-permute-start | bytes 786440 | tf_op jit(solution)/shard_map/while/body/eval_jaxpr/ppermute | solution.py:16
  829.8 11.9 %collective-permute-start.1 = (f32[4,128,128]{2,1,0:T(8,128)S(1)}, f32[4,128,128]{2,1,0:T(8,128)S(1)}, u32[]{:S(2)}, u32[]{:S(2)}) collective-permute-start(f32[4,128,128]{2,1,0:T(8,128)S(1)} %get-tuple-element.155), channel_id=1, source_target_pairs={{8,0},{16,8},{24,16},{32,24},{40,32},{48,40},{56,48},{64,56},{72,6... | collective-permute-start | bytes 786440 | tf_op jit(solution)/shard_map/while/body/eval_jaxpr/ppermute | solution.py:16
  841.8 11.6 %collective-permute-start.1 = (f32[4,128,128]{2,1,0:T(8,128)S(1)}, f32[4,128,128]{2,1,0:T(8,128)S(1)}, u32[]{:S(2)}, u32[]{:S(2)}) collective-permute-start(f32[4,128,128]{2,1,0:T(8,128)S(1)} %get-tuple-element.155), channel_id=1, source_target_pairs={{8,0},{16,8},{24,16},{32,24},{40,32},{48,40},{56,48},{64,56},{72,6... | collective-permute-start | bytes 786440 | tf_op jit(solution)/shard_map/while/body/eval_jaxpr/ppermute | solution.py:16
  853.5 11.6 %collective-permute-start.1 = (f32[4,128,128]{2,1,0:T(8,128)S(1)}, f32[4,128,128]{2,1,0:T(8,128)S(1)}, u32[]{:S(2)}, u32[]{:S(2)}) collective-permute-start(f32[4,128,128]{2,1,0:T(8,128)S(1)} %get-tuple-element.155), channel_id=1, source_target_pairs={{8,0},{16,8},{24,16},{32,24},{40,32},{48,40},{56,48},{64,56},{72,6... | collective-permute-start | bytes 786440 | tf_op jit(solution)/shard_map/while/body/eval_jaxpr/ppermute | solution.py:16
  865.3 11.6 %collective-permute-start.1 = (f32[4,128,128]{2,1,0:T(8,128)S(1)}, f32[4,128,128]{2,1,0:T(8,128)S(1)}, u32[]{:S(2)}, u32[]{:S(2)}) collective-permute-start(f32[4,128,128]{2,1,0:T(8,128)S(1)} %get-tuple-element.155), channel_id=1, source_target_pairs={{8,0},{16,8},{24,16},{32,24},{40,32},{48,40},{56,48},{64,56},{72,6... | collective-permute-start | bytes 786440 | tf_op jit(solution)/shard_map/while/body/eval_jaxpr/ppermute | solution.py:16
  (18 other events, 35.7 us)
where the time goes:
time: 900 us; the launch traced here: 897 us
  waiting for transfers between devices  466 us (52%)
  starting transfers between devices  292 us (32%)
  other arithmetic  61.7 us (7%)
  local copies, waits for them, and re-layouts  40.2 us (4%)
  matrix products  20.8 us (2%)
  blocking collectives  12.8 us (1%)
    ppermute x62, waiting for transfers between devices, passed_along(): return lax.ppermute(block, axis, route)  466 us
    ppermute x62, starting transfers between devices, passed_along(): return lax.ppermute(block, axis, route)  292 us
    add x31, other arithmetic, pass_lower(): return (moving, accum + moving)  51.3 us
    while x62, local copies, waits for them, and re-layouts  22.3 us
  transfers between devices with their start and end apart: 62, of which 62 were waited for; matrix products, arithmetic and copies ran while one was open for 0% of the time, Pallas kernels for 0%

commit v1 on v0

v1 whole, which is shorter than its diff:
```python
import functools

import jax
import jax.numpy as jnp
from jax import lax
from jax.experimental import pallas as pl
from jax.experimental.pallas import tpu as pltpu
from jax.sharding import PartitionSpec as P

HD = 128
BLK = 512
HALF = BLK // 2
EPS = 1e-06
SLICE = 8
MESH = pl.DeviceIdType.MESH

F32 = jnp.float32
BF16 = jnp.bfloat16

NN = (((1,), (0,)), ((), ()))
NT = (((1,), (1,)), ((), ()))
TN = (((0,), (0,)), ((), ()))


def dot(a, b, dims):
    return lax.dot_general(a, b, dims, preferred_element_type=F32)


def lower(rows, columns, offset):
    s = lax.broadcasted_iota(jnp.int32, (rows, columns), 0) + offset
    t = lax.broadcasted_iota(jnp.int32, (rows, columns), 1)
    return t <= s


def upper(rows, columns):
    t = lax.broadcasted_iota(jnp.int32, (rows, columns), 0)
    s = lax.broadcasted_iota(jnp.int32, (rows, columns), 1)
    return t <= s


def masked(scores, mask):
    return jnp.where(mask, scores, 0.0).astype(BF16)


def kernel(
    n_seq,
    n_head,
    width,
    q_hbm,
    k_hbm,
    v_hbm,
    gain_ref,
    g_hbm,
    normed_hbm,
    gq_hbm,
    gk_hbm,
    gv_hbm,
    q,
    k,
    v,
    g,
    num,
    dn,
    first,
    local,
    state,
    a_t,
    gk_part,
    gv_part,
    normed,
    gq,
    gk,
    gv,
    gathered,
    prefix,
    arrived,
    stats,
    all_stats,
    in_sem,
    out_sem,
    send_sem,
    recv_sem,
    stat_send,
    stat_recv,
):
    rows, columns = q.shape
    heads = columns // HD
    chunks = heads // 2
    blocks = rows // BLK
    seq = lax.axis_index("seq")
    head = lax.axis_index("head")
    seq_partners = [lax.rem(seq + d, n_seq) for d in range(1, n_seq)]
    head_partners = [lax.rem(head + d, n_head) for d in range(1, n_head)]

    def cols(c):
        return slice(c * 2 * HD, (c + 1) * 2 * HD)

    loads = {}
    for c in range(chunks):
        for i, (name, src, dst) in enumerate((("k", k_hbm, k), ("v", v_hbm, v))):
            loads[name, c] = pltpu.make_async_copy(
                src.at[:, cols(c)], dst.at[:, cols(c)], in_sem.at[2 * c + i]
            )
            loads[name, c].start()
    for i, (name, src, dst) in enumerate((("q", q_hbm, q), ("g", g_hbm, g))):
        loads[name] = pltpu.make_async_copy(src, dst, in_sem.at[2 * chunks + i])
        loads[name].start()

    barrier = pltpu.get_barrier_semaphore()
    for p in seq_partners:
        pl.semaphore_signal(barrier, inc=1, device_id=(p, head), device_id_type=MESH)
    for p in head_partners:
        pl.semaphore_signal(barrier, inc=1, device_id=(seq, p), device_id_type=MESH)

    def exchange(scan, phase, c, source, landing):
        at = ((scan * 2) + phase) * chunks + c
        for p in seq_partners:
            pltpu.make_async_remote_copy(
                src_ref=source(p),
                dst_ref=landing,
                send_sem=send_sem.at[at],
                recv_sem=recv_sem.at[at],
                device_id=(p, head),
                device_id_type=MESH,
            ).start()

    def wait_exchange(scan, phase, c):
        at = ((scan * 2) + phase) * chunks + c
        n = n_seq - 1
        pltpu.make_async_copy(
            gathered.at[scan, c, pl.ds(0, n)],
            gathered.at[scan, c, pl.ds(0, n)],
            recv_sem.at[at],
        ).wait()

    def wait_sent(scan, phase, c):
        at = ((scan * 2) + phase) * chunks + c
        n = n_seq - 1
        pltpu.make_async_copy(
            gathered.at[scan, c, pl.ds(0, n)],
            gathered.at[scan, c, pl.ds(0, n)],
            send_sem.at[at],
        ).wait()

    def scatter(scan, c):
        gathered[scan, c, seq] = local[scan, c, seq]
        exchange(
            scan, 0, c, lambda p: local.at[scan, c, p], gathered.at[scan, c, seq]
        )

    def scan_and_return(scan, c):
        wait_exchange(scan, 0, c)
        total = jnp.zeros((SLICE, HD), F32)
        order = range(n_seq) if scan == 0 else range(n_seq - 1, -1, -1)
        for j in order:
            prefix[scan, c, j] = total
            total = total + gathered[scan, c, j]
        arrived[scan, c, seq] = prefix[scan, c, seq]
        exchange(
            scan, 1, c, lambda p: prefix.at[scan, c, p], arrived.at[scan, c, seq]
        )

    def outer_products(scan, c, left, right, keep):
        for i in range(2):
            h = 2 * c + i
            lane = slice(h * HD, (h + 1) * HD)
            parts = [
                dot(left[b * BLK : (b + 1) * BLK, lane], right[b * BLK : (b + 1) * BLK, lane], TN)
                for b in range(blocks)
            ]
            first[scan, c, i] = parts[keep]
            per = HD // SLICE
            local[scan, c, i * per : (i + 1) * per] = (parts[0] + parts[1]).reshape(
                per, SLICE, HD
            )

    for c in range(chunks):
        loads["k", c].wait()
        loads["v", c].wait()
        outer_products(0, c, k, v, 0)
        if c == 0:
            pl.semaphore_wait(barrier, n_seq - 1 + n_head - 1)
        scatter(0, c)

    loads["q"].wait()

    def scores(i, _):
        h = i // blocks
        b = lax.rem(i, blocks)
        lane = pl.ds(pl.multiple_of(h * HD, HD), HD)
        r0 = pl.multiple_of(b * BLK, BLK)
        lo, hi, both = pl.ds(r0, HALF), pl.ds(r0 + HALF, HALF), pl.ds(r0, BLK)
        a0 = masked(dot(q[lo, lane], k[lo, lane], NT), lower(HALF, HALF, 0))
        a1 = masked(dot(q[hi, lane], k[both, lane], NT), lower(HALF, BLK, HALF))
        num[lo, lane] = dot(a0, v[lo, lane], NN)
        num[hi, lane] = dot(a1, v[both, lane], NN)
        t0 = masked(dot(k[lo, lane], q[both, lane], NT), upper(HALF, BLK))
        t1 = masked(dot(k[hi, lane], q[hi, lane], NT), upper(HALF, HALF))
        a_t[h, b, 0:HALF, :] = t0
        a_t[h, b, HALF:BLK, HALF:BLK] = t1
        return 0

    lax.fori_loop(0, heads * blocks, scores, 0)

    for c in range(chunks):
        scan_and_return(0, c)

    loads["g"].wait()
    square = [None] * blocks
    product = [None] * blocks
    for c in range(chunks):
        wait_exchange(0, 1, c)
        for i in range(2):
            h = 2 * c + i
            lane = slice(h * HD, (h + 1) * HD)
            per = HD // SLICE
            incoming = arrived[0, c, i * per : (i + 1) * per].reshape(HD, HD)
            for b in range(blocks):
                row = slice(b * BLK, (b + 1) * BLK)
                s_bf = (incoming if b == 0 else incoming + first[0, c, i]).astype(BF16)
                state[h, b] = s_bf
                n = num[row, lane] + dot(q[row, lane], s_bf, NN)
                num[row, lane] = n
                gn = g[row, lane].astype(F32) * gain_ref[:, lane]
                sq, pr = n * n, gn * n
                square[b] = sq if square[b] is None else square[b] + sq
                product[b] = pr if product[b] is None else product[b] + pr

    ones = jnp.ones((SLICE, HD), BF16)

    def across(x):
        hi = x.astype(BF16)
        rest = x - hi.astype(F32)
        mid = rest.astype(BF16)
        low = (rest - mid.astype(F32)).astype(BF16)
        return (dot(ones, hi, NT) + dot(ones, mid, NT) + dot(ones, low, NT))[0:1]

    for b in range(blocks):
        stats[b : b + 1, :] = across(square[b])
        stats[blocks + b : blocks + b + 1, :] = across(product[b])
    all_stats[head] = stats[...]
    for p in head_partners:
        pltpu.make_async_remote_copy(
            src_ref=stats,
            dst_ref=all_stats.at[head],
            send_sem=stat_send,
            recv_sem=stat_recv,
            device_id=(seq, p),
            device_id_type=MESH,
        ).start()

    def stat_wait(sem):
        view = all_stats.at[pl.ds(0, n_head - 1)]
        pltpu.make_async_copy(view, view, sem).wait()

    stat_wait(stat_recv)
    totals = all_stats[0]
    for j in range(1, n_head):
        totals = totals + all_stats[j]
    ratio = lax.rsqrt(totals[0:blocks] / width + EPS)
    inner = totals[blocks:] / width
    weight = ratio * ratio * inner
    packed = jnp.concatenate([ratio, weight, jnp.zeros((8 - 2 * blocks, BLK), F32)], axis=0)
    turned = jnp.transpose(packed)
    ratios = [jnp.broadcast_to(turned[:, b : b + 1], (BLK, HD)) for b in range(blocks)]
    weights = [
        jnp.broadcast_to(turned[:, blocks + b : blocks + b + 1], (BLK, HD))
        for b in range(blocks)
    ]

    for c in range(chunks):
        for i in range(2):
            lane = slice((2 * c + i) * HD, (2 * c + i + 1) * HD)
            for b in range(blocks):
                row = slice(b * BLK, (b + 1) * BLK)
                n = num[row, lane]
                gn = g[row, lane].astype(F32) * gain_ref[:, lane]
                dn[row, lane] = (ratios[b] * (gn - weights[b] * n)).astype(BF16)
                normed[row, lane] = (n * ratios[b] * gain_ref[:, lane]).astype(BF16)
        outer_products(1, c, q, dn, 1)
        scatter(1, c)

    outs = {}

    def write(at, src, dst):
        outs[at] = pltpu.make_async_copy(src, dst, out_sem.at[at])
        outs[at].start()

    write(0, normed, normed_hbm)

    def backward(i, _):
        h = i // blocks
        b = lax.rem(i, blocks)
        lane = pl.ds(pl.multiple_of(h * HD, HD), HD)
        r0 = pl.multiple_of(b * BLK, BLK)
        lo, hi, both = pl.ds(r0, HALF), pl.ds(r0 + HALF, HALF), pl.ds(r0, BLK)
        b0 = masked(dot(dn[lo, lane], v[lo, lane], NT), lower(HALF, HALF, 0))
        b1 = masked(dot(dn[hi, lane], v[both, lane], NT), lower(HALF, BLK, HALF))
        s_bf = state[h, b]
        gq[lo, lane] = (dot(b0, k[lo, lane], NN) + dot(dn[lo, lane], s_bf, NT)).astype(BF16)
        gq[hi, lane] = (dot(b1, k[both, lane], NN) + dot(dn[hi, lane], s_bf, NT)).astype(BF16)
        t0 = masked(dot(v[lo, lane], dn[both, lane], NT), upper(HALF, BLK))
        t1 = masked(dot(v[hi, lane], dn[hi, lane], NT), upper(HALF, HALF))
        gk_part[lo, lane] = dot(t0, q[both, lane], NN)
        gk_part[hi, lane] = dot(t1, q[hi, lane], NN)
        gv_part[lo, lane] = dot(a_t[h, b, 0:HALF, :], dn[both, lane], NN)
        gv_part[hi, lane] = dot(a_t[h, b, HALF:BLK, HALF:BLK], dn[hi, lane], NN)
        return 0

    lax.fori_loop(0, heads * blocks, backward, 0)
    write(1, gq, gq_hbm)

    for c in range(chunks):
        scan_and_return(1, c)

    for c in range(chunks):
        wait_exchange(1, 1, c)
        for i in range(2):
            h = 2 * c + i
            lane = slice(h * HD, (h + 1) * HD)
            per = HD // SLICE
            incoming = arrived[1, c, i * per : (i + 1) * per].reshape(HD, HD)
            for b in range(blocks):
                row = slice(b * BLK, (b + 1) * BLK)
                r_bf = (incoming if b == 1 else incoming + first[1, c, i]).astype(BF16)
                gk[row, lane] = (gk_part[row, lane] + dot(v[row, lane], r_bf, NT)).astype(BF16)
                gv[row, lane] = (gv_part[row, lane] + dot(k[row, lane], r_bf, NN)).astype(BF16)
        write(2 + 2 * c, gk.at[:, cols(c)], gk_hbm.at[:, cols(c)])
        write(3 + 2 * c, gv.at[:, cols(c)], gv_hbm.at[:, cols(c)])

    for scan in range(2):
        for phase in range(2):
            for c in range(chunks):
                wait_sent(scan, phase, c)
    stat_wait(stat_send)
    for copy in outs.values():
        copy.wait()


def shards(queries, keys, values, gain, grad_out):
    rows, columns = queries.shape
    heads = columns // HD
    chunks = heads // 2
    blocks = rows // BLK
    n_seq, n_head = lax.axis_size("seq"), lax.axis_size("head")
    out = jax.ShapeDtypeStruct((rows, columns), BF16)
    anywhere = pl.BlockSpec(memory_space=pl.ANY)
    big = pltpu.VMEM((rows, columns), BF16)
    wide = pltpu.VMEM((rows, columns), F32)
    pieces = pltpu.VMEM((2, chunks, n_seq, SLICE, HD), F32)
    flops = heads * blocks * (12 * BLK * BLK * HD + 12 * BLK * HD * HD)
    return pl.pallas_call(
        functools.partial(kernel, n_seq, n_head, columns * n_head),
        out_shape=(out, out, out, out),
        in_specs=[anywhere, anywhere, anywhere, pl.BlockSpec(memory_space=pltpu.VMEM), anywhere],
        out_specs=(anywhere, anywhere, anywhere, anywhere),
        scratch_shapes=[
            big,
            big,
            big,
            big,
            wide,
            big,
            pltpu.VMEM((2, chunks, 2, HD, HD), F32),
            pieces,
            pltpu.VMEM((heads, blocks, HD, HD), BF16),
            pltpu.VMEM((heads, blocks, BLK, BLK), BF16),
            wide,
            wide,
            big,
            big,
            big,
            big,
            pieces,
            pieces,
            pieces,
            pltpu.VMEM((2 * blocks, BLK), F32),
            pltpu.VMEM((n_head, 2 * blocks, BLK), F32),
            pltpu.SemaphoreType.DMA((2 * chunks + 2,)),
            pltpu.SemaphoreType.DMA((2 + 2 * chunks,)),
            pltpu.SemaphoreType.DMA((4 * chunks,)),
            pltpu.SemaphoreType.DMA((4 * chunks,)),
            pltpu.SemaphoreType.DMA,
            pltpu.SemaphoreType.DMA,
        ],
        compiler_params=pltpu.CompilerParams(
            collective_id=0, has_side_effects=True, vmem_limit_bytes=48 << 20
        ),
        cost_estimate=pl.CostEstimate(
            flops=flops, bytes_accessed=8 * rows * columns * 2, transcendentals=0
        ),
    )(queries, keys, values, gain.reshape(1, columns), grad_out)


def solution(mesh):
    spec = P("seq", "head")
    return jax.shard_map(
        shards,
        mesh=mesh,
        in_specs=(spec, spec, spec, P("head"), spec),
        out_specs=(spec, spec, spec, spec),
        check_vma=False,
    )
```

time: 900 us -> 58.6 us (0.07)
  the two profiles are of different devices: /device:TPU:102 before, /device:TPU:2 now
where the time goes in v1:
time: 58.6 us; the launch traced here: 58 us
  Pallas kernels  51.6 us (88%)
  local copies, waits for them, and re-layouts  5.78 us (10%)
  between operations  0.65 us (1%)
    pallas_call x1, Pallas kernels, shards(): pl.pallas_call(functools.partial(kernel, n_seq, n_head, columns * n_head)...  51.6 us
    unnamed x8, local copies, waits for them, and re-layouts  5.78 us

profile of v1, /device:TPU:2, one launch (start us, length us, event | category | flops | bytes accessed | tf_op | source)
XLA Modules:
  0.0 58.0 jit_solution(1692696133818064644)
XLA Ops:
  0.6 0.0 copy-start
  0.6 1.2 %copy-done = bf16[1024,512]{1,0:T(8,128)(2,1)S(1)} copy-done((bf16[1024,512]{1,0:T(8,128)(2,1)S(1)}, bf16[1024,512]{1,0:T(8,128)(2,1)}, u32[]{:S(2)}) %copy-start) | copy-done | bytes 1048600
  1.9 0.0 copy-start.1
  1.9 0.7 %copy-done.1 = f32[512]{0:T(512)S(1)} copy-done((f32[512]{0:T(512)S(1)}, f32[512]{0:T(512)}, u32[]{:S(2)}) %copy-start.1) | copy-done | bytes 2072
  2.5 51.6 %shard_map.84 = (bf16[1024,512]{1,0:T(8,128)(2,1)S(1)}, bf16[1024,512]{1,0:T(8,128)(2,1)S(1)}, bf16[1024,512]{1,0:T(8,128)(2,1)S(1)}, bf16[1024,512]{1,0:T(8,128)(2,1)S(1)}) custom-call(bf16[1024,512]{1,0:T(8,128)(2,1)S(1)} %copy-done, bf16[1024,512]{1,0:T(8,128)(2,1)} %k_hbm.1, bf16[1024,512]{1,0:T(8,128)(2,1)} %v_hbm.1, f32[1,512]{1,0:T(1,128)S(1)} %bitcast.1, ...), custom_call_target="tpu_custom_call" | custom-call | flops 4026531840 | bytes 8388608 | tf_op jit(solution)/shard_map/pallas_call | solution.py:352
  54.1 1.0 %copy.13 = bf16[1024,512]{1,0:T(8,128)(2,1)} copy(bf16[1024,512]{1,0:T(8,128)(2,1)S(1)} %get-tuple-element.8) | data formatting | bytes 2097152
  55.1 1.0 %copy.14 = bf16[1024,512]{1,0:T(8,128)(2,1)} copy(bf16[1024,512]{1,0:T(8,128)(2,1)S(1)} %get-tuple-element.9) | data formatting | bytes 2097152
  56.1 1.0 %copy.15 = bf16[1024,512]{1,0:T(8,128)(2,1)} copy(bf16[1024,512]{1,0:T(8,128)(2,1)S(1)} %get-tuple-element.10) | data formatting | bytes 2097152
  57.1 1.0 %copy.16 = bf16[1024,512]{1,0:T(8,128)(2,1)} copy(bf16[1024,512]{1,0:T(8,128)(2,1)S(1)} %get-tuple-element.11) | data formatting | bytes 2097152
Async XLA Ops:
  0.6 1.2 %copy-start = (bf16[1024,512]{1,0:T(8,128)(2,1)S(1)}, bf16[1024,512]{1,0:T(8,128)(2,1)}, u32[]{:S(2)}) copy-start(bf16[1024,512]{1,0:T(8,128)(2,1)} %q_hbm.1) | copy-start | bytes 3145732
  1.9 0.7 %copy-start.1 = (f32[512]{0:T(512)S(1)}, f32[512]{0:T(512)}, u32[]{:S(2)}) copy-start(f32[512]{0:T(512)} %param.8) | copy-start | bytes 6148

commit v2 on v1

--- a/solution.py
+++ b/solution.py
@@ -12,6 +12,8 @@
 HALF = BLK // 2
 EPS = 1e-06
 SLICE = 8
+X = 4
+CORES = 2
 MESH = pl.DeviceIdType.MESH
 
 F32 = jnp.float32
@@ -20,6 +22,20 @@
 NN = (((1,), (0,)), ((), ()))
 NT = (((1,), (1,)), ((), ()))
 TN = (((0,), (0,)), ((), ()))
+
+
+def far_first(me, n, inner):
+    outer = n // inner
+    major, minor = me // inner, lax.rem(me, inner)
+
+    def hops(step):
+        return min(step[0], outer - step[0]) + min(step[1], inner - step[1])
+
+    steps = [(i, j) for i in range(outer) for j in range(inner) if i + j]
+    return [
+        lax.rem(major + i, outer) * inner + lax.rem(minor + j, inner)
+        for i, j in sorted(steps, key=hops, reverse=True)
+    ]
 
 
 def dot(a, b, dims):
@@ -49,35 +65,30 @@
     q_hbm,
     k_hbm,
     v_hbm,
-    gain_ref,
+    gain_hbm,
     g_hbm,
-    normed_hbm,
-    gq_hbm,
-    gk_hbm,
-    gv_hbm,
-    q,
+    normed,
+    gq,
+    gk_part,
+    gv_part,
     k,
     v,
+    later,
+    q,
     g,
+    gain_ref,
     num,
     dn,
     first,
     local,
     state,
     a_t,
-    gk_part,
-    gv_part,
-    normed,
-    gq,
-    gk,
-    gv,
     gathered,
     prefix,
     arrived,
     stats,
     all_stats,
     in_sem,
-    out_sem,
     send_sem,
     recv_sem,
     stat_send,
@@ -89,11 +100,17 @@
     blocks = rows // BLK
     seq = lax.axis_index("seq")
     head = lax.axis_index("head")
-    seq_partners = [lax.rem(seq + d, n_seq) for d in range(1, n_seq)]
-    head_partners = [lax.rem(head + d, n_head) for d in range(1, n_head)]
+    seq_partners = far_first(seq, n_seq, X)
+    head_partners = far_first(head, n_head, CORES)
 
     def cols(c):
         return slice(c * 2 * HD, (c + 1) * 2 * HD)
+
+    barrier = pltpu.get_barrier_semaphore()
+    for p in seq_partners:
+        pl.semaphore_signal(barrier, inc=1, device_id=(p, head), device_id_type=MESH)
+    for p in head_partners:
+        pl.semaphore_signal(barrier, inc=1, device_id=(seq, p), device_id_type=MESH)
 
     loads = {}
     for c in range(chunks):
@@ -102,15 +119,11 @@
                 src.at[:, cols(c)], dst.at[:, cols(c)], in_sem.at[2 * c + i]
             )
             loads[name, c].start()
-    for i, (name, src, dst) in enumerate((("q", q_hbm, q), ("g", g_hbm, g))):
+    for i, (name, src, dst) in enumerate(
+        (("q", q_hbm, q), ("g", g_hbm, g), ("gain", gain_hbm, gain_ref))
+    ):
         loads[name] = pltpu.make_async_copy(src, dst, in_sem.at[2 * chunks + i])
         loads[name].start()
-
-    barrier = pltpu.get_barrier_semaphore()
-    for p in seq_partners:
-        pl.semaphore_signal(barrier, inc=1, device_id=(p, head), device_id_type=MESH)
-    for p in head_partners:
-        pl.semaphore_signal(barrier, inc=1, device_id=(seq, p), device_id_type=MESH)
 
     def exchange(scan, phase, c, source, landing):
         at = ((scan * 2) + phase) * chunks + c
@@ -206,6 +219,7 @@
         scan_and_return(0, c)
 
     loads["g"].wait()
+    loads["gain"].wait()
     square = [None] * blocks
     product = [None] * blocks
     for c in range(chunks):
@@ -279,14 +293,6 @@
                 normed[row, lane] = (n * ratios[b] * gain_ref[:, lane]).astype(BF16)
         outer_products(1, c, q, dn, 1)
         scatter(1, c)
-
-    outs = {}
-
-    def write(at, src, dst):
-        outs[at] = pltpu.make_async_copy(src, dst, out_sem.at[at])
-        outs[at].start()
-
-    write(0, normed, normed_hbm)
 
     def backward(i, _):
         h = i // blocks
@@ -307,33 +313,66 @@
         gv_part[hi, lane] = dot(a_t[h, b, HALF:BLK, HALF:BLK], dn[hi, lane], NN)
         return 0
 
-    lax.fori_loop(0, heads * blocks, backward, 0)
-    write(1, gq, gq_hbm)
+    lax.fori_loop(0, heads * blocks // 2, backward, 0)
 
     for c in range(chunks):
         scan_and_return(1, c)
+
+    lax.fori_loop(heads * blocks // 2, heads * blocks, backward, 0)
 
     for c in range(chunks):
         wait_exchange(1, 1, c)
         for i in range(2):
-            h = 2 * c + i
-            lane = slice(h * HD, (h + 1) * HD)
             per = HD // SLICE
             incoming = arrived[1, c, i * per : (i + 1) * per].reshape(HD, HD)
             for b in range(blocks):
-                row = slice(b * BLK, (b + 1) * BLK)
-                r_bf = (incoming if b == 1 else incoming + first[1, c, i]).astype(BF16)
-                gk[row, lane] = (gk_part[row, lane] + dot(v[row, lane], r_bf, NT)).astype(BF16)
-                gv[row, lane] = (gv_part[row, lane] + dot(k[row, lane], r_bf, NN)).astype(BF16)
-        write(2 + 2 * c, gk.at[:, cols(c)], gk_hbm.at[:, cols(c)])
-        write(3 + 2 * c, gv.at[:, cols(c)], gv_hbm.at[:, cols(c)])
+                r = incoming if b == 1 else incoming + first[1, c, i]
+                later[2 * c + i, b] = r.astype(BF16)
 
     for scan in range(2):
         for phase in range(2):
             for c in range(chunks):
                 wait_sent(scan, phase, c)
     stat_wait(stat_send)
-    for copy in outs.values():
+
+
+def finish(
+    normed,
+    gq,
+    gk_part,
+    gv_part,
+    k,
+    v,
+    later,
+    normed_hbm,
+    gq_hbm,
+    gk_hbm,
+    gv_hbm,
+    gk,
+    gv,
+    out_sem,
+):
+    rows, columns = k.shape
+    blocks = rows // BLK
+    outs = []
+
+    def write(src, dst):
+        outs.append(pltpu.make_async_copy(src, dst, out_sem.at[len(outs)]))
+        outs[-1].start()
+
+    write(normed, normed_hbm)
+    write(gq, gq_hbm)
+    for h in range(columns // HD):
+        lane = slice(h * HD, (h + 1) * HD)
+        for b in range(blocks):
+            row = slice(b * BLK, (b + 1) * BLK)
+            gk[row, lane] = (gk_part[row, lane] + dot(v[row, lane], later[h, b], NT)).astype(BF16)
+            gv[row, lane] = (gv_part[row, lane] + dot(k[row, lane], later[h, b], NN)).astype(BF16)
+        if h % 2 == 1:
+            pair = slice((h - 1) * HD, (h + 1) * HD)
+            write(gk.at[:, pair], gk_hbm.at[:, pair])
+            write(gv.at[:, pair], gv_hbm.at[:, pair])
+    for copy in outs:
         copy.wait()
 
 
@@ -349,47 +388,66 @@
     wide = pltpu.VMEM((rows, columns), F32)
     pieces = pltpu.VMEM((2, chunks, n_seq, SLICE, HD), F32)
     flops = heads * blocks * (12 * BLK * BLK * HD + 12 * BLK * HD * HD)
-    return pl.pallas_call(
+    vmem = pl.BlockSpec(memory_space=pltpu.VMEM)
+    hbm = [
+        pltpu.with_memory_space_constraint(x, pltpu.HBM)
+        for x in (queries, keys, values, gain.reshape(1, columns), grad_out)
+    ]
+    kept = (
+        pltpu.VMEM((rows, columns), BF16),
+        pltpu.VMEM((rows, columns), BF16),
+        pltpu.VMEM((rows, columns), F32),
+        pltpu.VMEM((rows, columns), F32),
+        pltpu.VMEM((rows, columns), BF16),
+        pltpu.VMEM((rows, columns), BF16),
+        pltpu.VMEM((heads, blocks, HD, HD), BF16),
+    )
+    held = pl.pallas_call(
         functools.partial(kernel, n_seq, n_head, columns * n_head),
-        out_shape=(out, out, out, out),
-        in_specs=[anywhere, anywhere, anywhere, pl.BlockSpec(memory_space=pltpu.VMEM), anywhere],
-        out_specs=(anywhere, anywhere, anywhere, anywhere),
+        out_shape=kept,
+        in_specs=[anywhere] * 5,
+        out_specs=(vmem,) * len(kept),
         scratch_shapes=[
             big,
             big,
-            big,
-            big,
+            pltpu.VMEM((1, columns), F32),
             wide,
             big,
             pltpu.VMEM((2, chunks, 2, HD, HD), F32),
             pieces,
             pltpu.VMEM((heads, blocks, HD, HD), BF16),
             pltpu.VMEM((heads, blocks, BLK, BLK), BF16),
-            wide,
-            wide,
-            big,
-            big,
-            big,
-            big,
             pieces,
             pieces,
             pieces,
             pltpu.VMEM((2 * blocks, BLK), F32),
             pltpu.VMEM((n_head, 2 * blocks, BLK), F32),
-            pltpu.SemaphoreType.DMA((2 * chunks + 2,)),
-            pltpu.SemaphoreType.DMA((2 + 2 * chunks,)),
+            pltpu.SemaphoreType.DMA((2 * chunks + 3,)),
             pltpu.SemaphoreType.DMA((4 * chunks,)),
             pltpu.SemaphoreType.DMA((4 * chunks,)),
             pltpu.SemaphoreType.DMA,
             pltpu.SemaphoreType.DMA,
         ],
         compiler_params=pltpu.CompilerParams(
-            collective_id=0, has_side_effects=True, vmem_limit_bytes=48 << 20
+            collective_id=0, has_side_effects=True, vmem_limit_bytes=32 << 20
         ),
         cost_estimate=pl.CostEstimate(
-            flops=flops, bytes_accessed=8 * rows * columns * 2, transcendentals=0
+            flops=flops, bytes_accessed=4 * rows * columns * 2, transcendentals=0
         ),
-    )(queries, keys, values, gain.reshape(1, columns), grad_out)
+    )(*hbm)
+    return pl.pallas_call(
+        finish,
+        out_shape=(out, out, out, out),
+        in_specs=[vmem] * len(kept),
+        out_specs=(anywhere,) * 4,
+        scratch_shapes=[big, big, pltpu.SemaphoreType.DMA((2 + 2 * chunks,))],
+        compiler_params=pltpu.CompilerParams(vmem_limit_bytes=24 << 20),
+        cost_estimate=pl.CostEstimate(
+            flops=heads * blocks * 4 * BLK * HD * HD,
+            bytes_accessed=4 * rows * columns * 2,
+            transcendentals=0,
+        ),
+    )(*held)
 
 
 def solution(mesh):

time: 58.6 us -> 49.7 us (0.85)
  local copies, waits for them, and re-layouts: 5.78 us -> 0 us
  Pallas kernels: 51.6 us -> 48.6 us
    unnamed x8 -> x0, local copies, waits for them, and re-layouts: 5.78 us -> none
    pallas_call x1, Pallas kernels: 51.6 us -> 46.5 us  [shards(): pl.pallas_call(functools.partial(kernel, n_seq, n_head, columns * n_head)...]
    pallas_call x0 -> x1, Pallas kernels: none -> 2.06 us  [shards(): pl.pallas_call(finish, out_shape=(out, out, out, out), in_specs=[vmem] *...]
where the time goes in v2:
time: 49.7 us; the launch traced here: 49.2 us
  Pallas kernels  48.6 us (98%)
  between operations  0.64 us (1%)
    pallas_call x1, Pallas kernels, shards(): pl.pallas_call(functools.partial(kernel, n_seq, n_head, columns * n_head)...  46.5 us
    pallas_call x1, Pallas kernels, shards(): pl.pallas_call(finish, out_shape=(out, out, out, out), in_specs=[vmem] *...  2.06 us

profile of v2, /device:TPU:2, one launch (start us, length us, event | category | flops | bytes accessed | tf_op | source)
XLA Modules:
  0.0 49.2 jit_solution(5531171727896474044)
XLA Ops:
  0.6 46.5 %shard_map.84 = (bf16[1024,512]{1,0:T(8,128)(2,1)S(1)}, bf16[1024,512]{1,0:T(8,128)(2,1)S(1)}, f32[1024,512]{1,0:T(8,128)S(1)}, f32[1024,512]{1,0:T(8,128)S(1)},...) custom-call(bf16[1024,512]{1,0:T(8,128)(2,1)} %q_hbm.1, ...), custom_call_target="tpu_custom_call" | custom-call | flops 4026531840 | bytes 4194304 | tf_op jit(solution)/shard_map/pallas_call | solution.py:405
  47.2 2.1 %shard_map.85 = (bf16[1024,512]{1,0:T(8,128)(2,1)}, bf16[1024,512]{1,0:T(8,128)(2,1)}, bf16[1024,512]{1,0:T(8,128)(2,1)}, bf16[1024,512]{1,0:T(8,128)(2,1)}) custom-call(bf16[1024,512]{1,0:T(8,128)(2,1)S(1)} %get-tuple-element.11.normed, bf16[1024,512]{1,0:T(8,128)(2,1)S(1)} %get-tuple-element.12.gq, f32[1024,512]{1,0:T(8,128)S(1)} %get-tuple-element.13.gk_part, ...), custom_call_target="tpu_custom_call" | custom-call | flops 268435456 | bytes 4194304 | tf_op jit(solution)/shard_map/pallas_call | solution.py:438

commit v3 on v2

--- a/solution.py
+++ b/solution.py
@@ -56,6 +56,11 @@
 
 def masked(scores, mask):
     return jnp.where(mask, scores, 0.0).astype(BF16)
+
+
+def last_products(row, lane, r, v, k, gk_part, gv_part, gk, gv):
+    gk[row, lane] = (gk_part[row, lane] + dot(v[row, lane], r, NT)).astype(BF16)
+    gv[row, lane] = (gv_part[row, lane] + dot(k[row, lane], r, NN)).astype(BF16)
 
 
 def kernel(
@@ -69,6 +74,8 @@
     g_hbm,
     normed,
     gq,
+    gk,
+    gv,
     gk_part,
     gv_part,
     k,
@@ -77,11 +84,14 @@
     q,
     g,
     gain_ref,
+    gn,
+    q_t,
     num,
     dn,
     first,
     local,
     state,
+    pair,
     a_t,
     gathered,
     prefix,
@@ -173,24 +183,39 @@
             scan, 1, c, lambda p: prefix.at[scan, c, p], arrived.at[scan, c, seq]
         )
 
-    def outer_products(scan, c, left, right, keep):
+    def place_states(scan, c, b, plain):
+        per = HD // SLICE
+        for i in range(2):
+            at = slice(i * HD, (i + 1) * HD)
+            s = arrived[scan, c, i * per : (i + 1) * per].reshape(HD, HD)
+            s = s if plain else s + first[scan, c, i]
+            pair[scan, c, b, at, at] = s.astype(BF16)
+
+    def outer_products(scan, c, product_of, keep):
         for i in range(2):
             h = 2 * c + i
-            lane = slice(h * HD, (h + 1) * HD)
-            parts = [
-                dot(left[b * BLK : (b + 1) * BLK, lane], right[b * BLK : (b + 1) * BLK, lane], TN)
-                for b in range(blocks)
-            ]
+            parts = [product_of(h, b) for b in range(blocks)]
             first[scan, c, i] = parts[keep]
             per = HD // SLICE
             local[scan, c, i * per : (i + 1) * per] = (parts[0] + parts[1]).reshape(
                 per, SLICE, HD
             )
 
+    def tile(h, b):
+        return slice(b * BLK, (b + 1) * BLK), slice(h * HD, (h + 1) * HD)
+
+    def kv_product(h, b):
+        return dot(k[tile(h, b)], v[tile(h, b)], TN)
+
+    def qd_product(h, b):
+        row, lane = tile(h, b)
+        return dot(q_t[lane, row], dn[row, lane], NN)
+
+    pair[...] = jnp.zeros_like(pair)
     for c in range(chunks):
         loads["k", c].wait()
         loads["v", c].wait()
-        outer_products(0, c, k, v, 0)
+        outer_products(0, c, kv_product, 0)
         if c == 0:
             pl.semaphore_wait(barrier, n_seq - 1 + n_head - 1)
         scatter(0, c)
@@ -209,6 +234,7 @@
         num[hi, lane] = dot(a1, v[both, lane], NN)
         t0 = masked(dot(k[lo, lane], q[both, lane], NT), upper(HALF, BLK))
         t1 = masked(dot(k[hi, lane], q[hi, lane], NT), upper(HALF, HALF))
+        q_t[lane, both] = jnp.transpose(q[both, lane])
         a_t[h, b, 0:HALF, :] = t0
         a_t[h, b, HALF:BLK, HALF:BLK] = t1
         return 0
@@ -220,38 +246,29 @@
 
     loads["g"].wait()
     loads["gain"].wait()
+    gn[...] = g[...].astype(F32) * gain_ref[...]
     square = [None] * blocks
     product = [None] * blocks
     for c in range(chunks):
         wait_exchange(0, 1, c)
-        for i in range(2):
-            h = 2 * c + i
-            lane = slice(h * HD, (h + 1) * HD)
-            per = HD // SLICE
-            incoming = arrived[0, c, i * per : (i + 1) * per].reshape(HD, HD)
-            for b in range(blocks):
-                row = slice(b * BLK, (b + 1) * BLK)
-                s_bf = (incoming if b == 0 else incoming + first[0, c, i]).astype(BF16)
-                state[h, b] = s_bf
-                n = num[row, lane] + dot(q[row, lane], s_bf, NN)
-                num[row, lane] = n
-                gn = g[row, lane].astype(F32) * gain_ref[:, lane]
-                sq, pr = n * n, gn * n
-                square[b] = sq if square[b] is None else square[b] + sq
-                product[b] = pr if product[b] is None else product[b] + pr
-
-    ones = jnp.ones((SLICE, HD), BF16)
-
-    def across(x):
-        hi = x.astype(BF16)
-        rest = x - hi.astype(F32)
-        mid = rest.astype(BF16)
-        low = (rest - mid.astype(F32)).astype(BF16)
-        return (dot(ones, hi, NT) + dot(ones, mid, NT) + dot(ones, low, NT))[0:1]
-
-    for b in range(blocks):
-        stats[b : b + 1, :] = across(square[b])
-        stats[blocks + b : blocks + b + 1, :] = across(product[b])
+        for b in range(blocks):
+            place_states(0, c, b, b == 0)
+            for i in range(2):
+                at = slice(i * HD, (i + 1) * HD)
+                state[2 * c + i, b] = pair[0, c, b, at, at]
+            row = slice(b * BLK, (b + 1) * BLK)
+            n = num[row, cols(c)] + dot(q[row, cols(c)], pair[0, c, b], NN)
+            num[row, cols(c)] = n
+            sq, pr = n * n, gn[row, cols(c)] * n
+            sq, pr = sq[:, :HD] + sq[:, HD:], pr[:, :HD] + pr[:, HD:]
+            square[b] = sq if c == 0 else square[b] + sq
+            product[b] = pr if c == 0 else product[b] + pr
+
+    lanes = lax.broadcasted_iota(jnp.int32, (BLK, HD), 1)
+    mixed = jnp.zeros((BLK, HD), F32)
+    for at, x in enumerate(square + product):
+        mixed = jnp.where(lanes == at, jnp.sum(x, axis=1, keepdims=True), mixed)
+    stats[...] = jnp.transpose(mixed)[0 : 2 * blocks]
     all_stats[head] = stats[...]
     for p in head_partners:
         pltpu.make_async_remote_copy(
@@ -284,15 +301,16 @@
 
     for c in range(chunks):
         for i in range(2):
-            lane = slice((2 * c + i) * HD, (2 * c + i + 1) * HD)
             for b in range(blocks):
-                row = slice(b * BLK, (b + 1) * BLK)
-                n = num[row, lane]
-                gn = g[row, lane].astype(F32) * gain_ref[:, lane]
-                dn[row, lane] = (ratios[b] * (gn - weights[b] * n)).astype(BF16)
-                normed[row, lane] = (n * ratios[b] * gain_ref[:, lane]).astype(BF16)
-        outer_products(1, c, q, dn, 1)
+                at = tile(2 * c + i, b)
+                dn[at] = (ratios[b] * (gn[at] - weights[b] * num[at])).astype(BF16)
+        outer_products(1, c, qd_product, 1)
         scatter(1, c)
+
+    for h in range(heads):
+        for b in range(blocks):
+            row, lane = tile(h, b)
+            normed[row, lane] = (num[row, lane] * ratios[b] * gain_ref[:, lane]).astype(BF16)
 
     def backward(i, _):
         h = i // blocks
@@ -322,12 +340,15 @@
 
     for c in range(chunks):
         wait_exchange(1, 1, c)
-        for i in range(2):
-            per = HD // SLICE
-            incoming = arrived[1, c, i * per : (i + 1) * per].reshape(HD, HD)
-            for b in range(blocks):
-                r = incoming if b == 1 else incoming + first[1, c, i]
-                later[2 * c + i, b] = r.astype(BF16)
+        for b in range(blocks):
+            place_states(1, c, b, b == blocks - 1)
+            if c < chunks - 1:
+                row = slice(b * BLK, (b + 1) * BLK)
+                last_products(
+                    row, cols(c), pair[1, c, b], v, k, gk_part, gv_part, gk, gv
+                )
+            else:
+                later[b] = pair[1, c, b]
 
     for scan in range(2):
         for phase in range(2):
@@ -339,6 +360,8 @@
 def finish(
     normed,
     gq,
+    gk_done,
+    gv_done,
     gk_part,
     gv_part,
     k,
@@ -354,6 +377,8 @@
 ):
     rows, columns = k.shape
     blocks = rows // BLK
+    done = slice(0, columns - 2 * HD)
+    rest = slice(columns - 2 * HD, columns)
     outs = []
 
     def write(src, dst):
@@ -362,16 +387,13 @@
 
     write(normed, normed_hbm)
     write(gq, gq_hbm)
-    for h in range(columns // HD):
-        lane = slice(h * HD, (h + 1) * HD)
-        for b in range(blocks):
-            row = slice(b * BLK, (b + 1) * BLK)
-            gk[row, lane] = (gk_part[row, lane] + dot(v[row, lane], later[h, b], NT)).astype(BF16)
-            gv[row, lane] = (gv_part[row, lane] + dot(k[row, lane], later[h, b], NN)).astype(BF16)
-        if h % 2 == 1:
-            pair = slice((h - 1) * HD, (h + 1) * HD)
-            write(gk.at[:, pair], gk_hbm.at[:, pair])
-            write(gv.at[:, pair], gv_hbm.at[:, pair])
+    write(gk_done.at[:, done], gk_hbm.at[:, done])
+    write(gv_done.at[:, done], gv_hbm.at[:, done])
+    for b in range(blocks):
+        row = slice(b * BLK, (b + 1) * BLK)
+        last_products(row, rest, later[b], v, k, gk_part, gv_part, gk, gv)
+        write(gk.at[row, rest], gk_hbm.at[row, rest])
+        write(gv.at[row, rest], gv_hbm.at[row, rest])
     for copy in outs:
         copy.wait()
 
@@ -396,11 +418,13 @@
     kept = (
         pltpu.VMEM((rows, columns), BF16),
         pltpu.VMEM((rows, columns), BF16),
+        pltpu.VMEM((rows, columns), BF16),
+        pltpu.VMEM((rows, columns), BF16),
         pltpu.VMEM((rows, columns), F32),
         pltpu.VMEM((rows, columns), F32),
         pltpu.VMEM((rows, columns), BF16),
         pltpu.VMEM((rows, columns), BF16),
-        pltpu.VMEM((heads, blocks, HD, HD), BF16),
+        pltpu.VMEM((blocks, 2 * HD, 2 * HD), BF16),
     )
     held = pl.pallas_call(
         functools.partial(kernel, n_seq, n_head, columns * n_head),
@@ -412,10 +436,13 @@
             big,
             pltpu.VMEM((1, columns), F32),
             wide,
+            pltpu.VMEM((columns, rows), BF16),
+            wide,
             big,
             pltpu.VMEM((2, chunks, 2, HD, HD), F32),
             pieces,
             pltpu.VMEM((heads, blocks, HD, HD), BF16),
+            pltpu.VMEM((2, chunks, blocks, 2 * HD, 2 * HD), BF16),
             pltpu.VMEM((heads, blocks, BLK, BLK), BF16),
             pieces,
             pieces,
@@ -440,7 +467,7 @@
         out_shape=(out, out, out, out),
         in_specs=[vmem] * len(kept),
         out_specs=(anywhere,) * 4,
-        scratch_shapes=[big, big, pltpu.SemaphoreType.DMA((2 + 2 * chunks,))],
+        scratch_shapes=[big, big, pltpu.SemaphoreType.DMA((4 + 2 * blocks,))],
         compiler_params=pltpu.CompilerParams(vmem_limit_bytes=24 << 20),
         cost_estimate=pl.CostEstimate(
             flops=heads * blocks * 4 * BLK * HD * HD,

time: 49.7 us -> 49.4 us (level)
  no operation moved by 1% of the time
where the time goes in v3:
time: 49.4 us; the launch traced here: 48.9 us
  Pallas kernels  48.3 us (98%)
  between operations  0.64 us (1%)
    pallas_call x1, Pallas kernels, shards(): pl.pallas_call(functools.partial(kernel, n_seq, n_head, columns * n_head)...  46.2 us
    pallas_call x1, Pallas kernels, shards(): pl.pallas_call(finish, out_shape=(out, out, out, out), in_specs=[vmem] *...  2.08 us

profile of v3, /device:TPU:2, one launch (start us, length us, event | category | flops | bytes accessed | tf_op | source)
XLA Modules:
  0.0 48.9 jit_solution(1210986535019485018)
XLA Ops:
  0.6 46.2 %shard_map.84 = (bf16[1024,512]{1,0:T(8,128)(2,1)S(1)}, bf16[1024,512]{1,0:T(8,128)(2,1)S(1)}, bf16[1024,512]{1,0:T(8,128)(2,1)S(1)}, bf16[1024,512]{1,0:T(8,128...) custom-call(bf16[1024,512]{1,0:T(8,128)(2,1)} %q_hbm.1, ...), custom_call_target="tpu_custom_call" | custom-call | flops 4026531840 | bytes 4194304 | tf_op jit(solution)/shard_map/pallas_call | solution.py:429
  46.8 2.1 %shard_map.85 = (bf16[1024,512]{1,0:T(8,128)(2,1)}, bf16[1024,512]{1,0:T(8,128)(2,1)}, bf16[1024,512]{1,0:T(8,128)(2,1)}, bf16[1024,512]{1,0:T(8,128)(2,1)}) custom-call(bf16[1024,512]{1,0:T(8,128)(2,1)S(1)} %get-tuple-element.13.normed, bf16[1024,512]{1,0:T(8,128)(2,1)S(1)} %get-tuple-element.14.gq, bf16[1024,512]{1,0:T(8,128)(2,1)S(1)} %get-tuple-element.15.gk_done, ...), custom_call_target="tpu_custom_call" | custom-call | flops 268435456 | bytes 4194304 | tf_op jit(solution)/shard_map/pallas_call | solution.py:465

commit v4 on v3

--- a/solution.py
+++ b/solution.py
@@ -11,7 +11,8 @@
 BLK = 512
 HALF = BLK // 2
 EPS = 1e-06
-SLICE = 8
+GROUP = 8
+SLICE = 2 * HD // GROUP
 X = 4
 CORES = 2
 MESH = pl.DeviceIdType.MESH
@@ -96,6 +97,7 @@
     gathered,
     prefix,
     arrived,
+    totals,
     stats,
     all_stats,
     in_sem,
@@ -110,15 +112,22 @@
     blocks = rows // BLK
     seq = lax.axis_index("seq")
     head = lax.axis_index("head")
-    seq_partners = far_first(seq, n_seq, X)
+    n_group = n_seq // GROUP
+    group, member = seq // GROUP, lax.rem(seq, GROUP)
+    near_partners = far_first(member, GROUP, X)
+    far_partners = far_first(group, n_group, 1)
     head_partners = far_first(head, n_head, CORES)
 
     def cols(c):
         return slice(c * 2 * HD, (c + 1) * 2 * HD)
 
     barrier = pltpu.get_barrier_semaphore()
-    for p in seq_partners:
-        pl.semaphore_signal(barrier, inc=1, device_id=(p, head), device_id_type=MESH)
+    for p in far_partners:
+        to = (p * GROUP + member, head)
+        pl.semaphore_signal(barrier, inc=1, device_id=to, device_id_type=MESH)
+    for p in near_partners:
+        to = (group * GROUP + p, head)
+        pl.semaphore_signal(barrier, inc=1, device_id=to, device_id_type=MESH)
     for p in head_partners:
         pl.semaphore_signal(barrier, inc=1, device_id=(seq, p), device_id_type=MESH)
 
@@ -135,53 +144,60 @@
         loads[name] = pltpu.make_async_copy(src, dst, in_sem.at[2 * chunks + i])
         loads[name].start()
 
-    def exchange(scan, phase, c, source, landing):
-        at = ((scan * 2) + phase) * chunks + c
-        for p in seq_partners:
-            pltpu.make_async_remote_copy(
-                src_ref=source(p),
-                dst_ref=landing,
-                send_sem=send_sem.at[at],
-                recv_sem=recv_sem.at[at],
-                device_id=(p, head),
-                device_id_type=MESH,
-            ).start()
+    def sems(scan, phase, c):
+        return (scan * 3 + phase) * chunks + c
+
+    def send(scan, phase, c, source, landing, to):
+        at = sems(scan, phase, c)
+        pltpu.make_async_remote_copy(
+            src_ref=source,
+            dst_ref=landing,
+            send_sem=send_sem.at[at],
+            recv_sem=recv_sem.at[at],
+            device_id=(to, head),
+            device_id_type=MESH,
+        ).start()
+
+    def wait_for(sem, scan, phase, c):
+        n = (n_group if phase == 1 else GROUP) - 1
+        view = gathered.at[scan, c, pl.ds(0, n)]
+        pltpu.make_async_copy(view, view, sem.at[sems(scan, phase, c)]).wait()
 
     def wait_exchange(scan, phase, c):
-        at = ((scan * 2) + phase) * chunks + c
-        n = n_seq - 1
-        pltpu.make_async_copy(
-            gathered.at[scan, c, pl.ds(0, n)],
-            gathered.at[scan, c, pl.ds(0, n)],
-            recv_sem.at[at],
-        ).wait()
+        wait_for(recv_sem, scan, phase, c)
 
     def wait_sent(scan, phase, c):
-        at = ((scan * 2) + phase) * chunks + c
-        n = n_seq - 1
-        pltpu.make_async_copy(
-            gathered.at[scan, c, pl.ds(0, n)],
-            gathered.at[scan, c, pl.ds(0, n)],
-            send_sem.at[at],
-        ).wait()
+        wait_for(send_sem, scan, phase, c)
 
     def scatter(scan, c):
-        gathered[scan, c, seq] = local[scan, c, seq]
-        exchange(
-            scan, 0, c, lambda p: local.at[scan, c, p], gathered.at[scan, c, seq]
-        )
-
-    def scan_and_return(scan, c):
+        landing = gathered.at[scan, c, member]
+        for p in near_partners:
+            send(scan, 0, c, local.at[scan, c, p], landing, group * GROUP + p)
+        gathered[scan, c, member] = local[scan, c, member]
+
+    def share_totals(scan, c):
         wait_exchange(scan, 0, c)
-        total = jnp.zeros((SLICE, HD), F32)
-        order = range(n_seq) if scan == 0 else range(n_seq - 1, -1, -1)
-        for j in order:
-            prefix[scan, c, j] = total
-            total = total + gathered[scan, c, j]
-        arrived[scan, c, seq] = prefix[scan, c, seq]
-        exchange(
-            scan, 1, c, lambda p: prefix.at[scan, c, p], arrived.at[scan, c, seq]
-        )
+        sum_here = jnp.zeros((SLICE, HD), F32)
+        for j in range(GROUP) if scan == 0 else range(GROUP - 1, -1, -1):
+            prefix[scan, c, j] = sum_here
+            sum_here = sum_here + gathered[scan, c, j]
+        totals[scan, c, group] = sum_here
+        mine = totals.at[scan, c, group]
+        for p in far_partners:
+            send(scan, 1, c, mine, mine, p * GROUP + member)
+
+    def hand_back(scan, c):
+        wait_exchange(scan, 1, c)
+        outside = jnp.zeros((SLICE, HD), F32)
+        for j in range(n_group):
+            counts = j < group if scan == 0 else j > group
+            outside = outside + jnp.where(counts, totals[scan, c, j], 0.0)
+        for j in range(GROUP):
+            prefix[scan, c, j] = prefix[scan, c, j] + outside
+        landing = arrived.at[scan, c, member]
+        for p in near_partners:
+            send(scan, 2, c, prefix.at[scan, c, p], landing, group * GROUP + p)
+        arrived[scan, c, member] = prefix[scan, c, member]
 
     def place_states(scan, c, b, plain):
         per = HD // SLICE
@@ -217,7 +233,7 @@
         loads["v", c].wait()
         outer_products(0, c, kv_product, 0)
         if c == 0:
-            pl.semaphore_wait(barrier, n_seq - 1 + n_head - 1)
+            pl.semaphore_wait(barrier, n_group + GROUP + n_head - 3)
         scatter(0, c)
 
     loads["q"].wait()
@@ -239,10 +255,12 @@
         a_t[h, b, HALF:BLK, HALF:BLK] = t1
         return 0
 
-    lax.fori_loop(0, heads * blocks, scores, 0)
-
-    for c in range(chunks):
-        scan_and_return(0, c)
+    lax.fori_loop(0, heads * blocks // 2, scores, 0)
+    for c in range(chunks):
+        share_totals(0, c)
+    lax.fori_loop(heads * blocks // 2, heads * blocks, scores, 0)
+    for c in range(chunks):
+        hand_back(0, c)
 
     loads["g"].wait()
     loads["gain"].wait()
@@ -250,7 +268,7 @@
     square = [None] * blocks
     product = [None] * blocks
     for c in range(chunks):
-        wait_exchange(0, 1, c)
+        wait_exchange(0, 2, c)
         for b in range(blocks):
             place_states(0, c, b, b == 0)
             for i in range(2):
@@ -285,11 +303,11 @@
         pltpu.make_async_copy(view, view, sem).wait()
 
     stat_wait(stat_recv)
-    totals = all_stats[0]
+    whole = all_stats[0]
     for j in range(1, n_head):
-        totals = totals + all_stats[j]
-    ratio = lax.rsqrt(totals[0:blocks] / width + EPS)
-    inner = totals[blocks:] / width
+        whole = whole + all_stats[j]
+    ratio = lax.rsqrt(whole[0:blocks] / width + EPS)
+    inner = whole[blocks:] / width
     weight = ratio * ratio * inner
     packed = jnp.concatenate([ratio, weight, jnp.zeros((8 - 2 * blocks, BLK), F32)], axis=0)
     turned = jnp.transpose(packed)
@@ -331,15 +349,17 @@
         gv_part[hi, lane] = dot(a_t[h, b, HALF:BLK, HALF:BLK], dn[hi, lane], NN)
         return 0
 
-    lax.fori_loop(0, heads * blocks // 2, backward, 0)
-
-    for c in range(chunks):
-        scan_and_return(1, c)
-
-    lax.fori_loop(heads * blocks // 2, heads * blocks, backward, 0)
-
-    for c in range(chunks):
-        wait_exchange(1, 1, c)
+    steps = heads * blocks
+    lax.fori_loop(0, 3 * steps // 8, backward, 0)
+    for c in range(chunks):
+        share_totals(1, c)
+    lax.fori_loop(3 * steps // 8, 6 * steps // 8, backward, 0)
+    for c in range(chunks):
+        hand_back(1, c)
+    lax.fori_loop(6 * steps // 8, steps, backward, 0)
+
+    for c in range(chunks):
+        wait_exchange(1, 2, c)
         for b in range(blocks):
             place_states(1, c, b, b == blocks - 1)
             if c < chunks - 1:
@@ -351,7 +371,7 @@
                 later[b] = pair[1, c, b]
 
     for scan in range(2):
-        for phase in range(2):
+        for phase in range(3):
             for c in range(chunks):
                 wait_sent(scan, phase, c)
     stat_wait(stat_send)
@@ -408,7 +428,7 @@
     anywhere = pl.BlockSpec(memory_space=pl.ANY)
     big = pltpu.VMEM((rows, columns), BF16)
     wide = pltpu.VMEM((rows, columns), F32)
-    pieces = pltpu.VMEM((2, chunks, n_seq, SLICE, HD), F32)
+    pieces = pltpu.VMEM((2, chunks, GROUP, SLICE, HD), F32)
     flops = heads * blocks * (12 * BLK * BLK * HD + 12 * BLK * HD * HD)
     vmem = pl.BlockSpec(memory_space=pltpu.VMEM)
     hbm = [
@@ -447,11 +467,12 @@
             pieces,
             pieces,
             pieces,
+            pltpu.VMEM((2, chunks, n_seq // GROUP, SLICE, HD), F32),
             pltpu.VMEM((2 * blocks, BLK), F32),
             pltpu.VMEM((n_head, 2 * blocks, BLK), F32),
             pltpu.SemaphoreType.DMA((2 * chunks + 3,)),
-            pltpu.SemaphoreType.DMA((4 * chunks,)),
-            pltpu.SemaphoreType.DMA((4 * chunks,)),
+            pltpu.SemaphoreType.DMA((6 * chunks,)),
+            pltpu.SemaphoreType.DMA((6 * chunks,)),
             pltpu.SemaphoreType.DMA,
             pltpu.SemaphoreType.DMA,
         ],

time: 49.4 us -> 45.5 us (0.921)
  Pallas kernels: 48.3 us -> 44.8 us
    pallas_call x1, Pallas kernels: 46.2 us -> 42.7 us  [shards(): pl.pallas_call(functools.partial(kernel, n_seq, n_head, columns * n_head)...]
where the time goes in v4:
time: 45.5 us; the launch traced here: 45.4 us
  Pallas kernels  44.8 us (98%)
  between operations  0.64 us (1%)
    pallas_call x1, Pallas kernels, shards(): pl.pallas_call(functools.partial(kernel, n_seq, n_head, columns * n_head)...  42.7 us
    pallas_call x1, Pallas kernels, shards(): pl.pallas_call(finish, out_shape=(out, out, out, out), in_specs=[vmem] *...  2.08 us

profile of v4, /device:TPU:2, one launch (start us, length us, event | category | flops | bytes accessed | tf_op | source)
XLA Modules:
  0.0 45.4 jit_solution(3094806770343834454)
XLA Ops:
  0.6 42.7 %shard_map.84 = (bf16[1024,512]{1,0:T(8,128)(2,1)S(1)}, bf16[1024,512]{1,0:T(8,128)(2,1)S(1)}, bf16[1024,512]{1,0:T(8,128)(2,1)S(1)}, bf16[1024,512]{1,0:T(8,128...) custom-call(bf16[1024,512]{1,0:T(8,128)(2,1)} %q_hbm.1, ...), custom_call_target="tpu_custom_call" | custom-call | flops 4026531840 | bytes 4194304 | tf_op jit(solution)/shard_map/pallas_call | solution.py:449
  43.3 2.1 %shard_map.85 = (bf16[1024,512]{1,0:T(8,128)(2,1)}, bf16[1024,512]{1,0:T(8,128)(2,1)}, bf16[1024,512]{1,0:T(8,128)(2,1)}, bf16[1024,512]{1,0:T(8,128)(2,1)}) custom-call(bf16[1024,512]{1,0:T(8,128)(2,1)S(1)} %get-tuple-element.13.normed, bf16[1024,512]{1,0:T(8,128)(2,1)S(1)} %get-tuple-element.14.gq, bf16[1024,512]{1,0:T(8,128)(2,1)S(1)} %get-tuple-element.15.gk_done, ...), custom_call_target="tpu_custom_call" | custom-call | flops 268435456 | bytes 4194304 | tf_op jit(solution)/shard_map/pallas_call | solution.py:486

commit v5 on v4

--- a/solution.py
+++ b/solution.py
@@ -12,7 +12,7 @@
 HALF = BLK // 2
 EPS = 1e-06
 GROUP = 8
-SLICE = 2 * HD // GROUP
+SLICE = HD // GROUP
 X = 4
 CORES = 2
 MESH = pl.DeviceIdType.MESH
@@ -97,12 +97,16 @@
     gathered,
     prefix,
     arrived,
+    here,
     totals,
     stats,
     all_stats,
     in_sem,
     send_sem,
     recv_sem,
+    far_send_sem,
+    far_recv_sem,
+    entered,
     stat_send,
     stat_recv,
 ):
@@ -123,8 +127,12 @@
 
     barrier = pltpu.get_barrier_semaphore()
     for p in far_partners:
-        to = (p * GROUP + member, head)
-        pl.semaphore_signal(barrier, inc=1, device_id=to, device_id_type=MESH)
+
+        @pl.when(p > group)
+        def _():
+            to = (p * GROUP + member, head)
+            pl.semaphore_signal(barrier, inc=1, device_id=to, device_id_type=MESH)
+
     for p in near_partners:
         to = (group * GROUP + p, head)
         pl.semaphore_signal(barrier, inc=1, device_id=to, device_id_type=MESH)
@@ -144,78 +152,97 @@
         loads[name] = pltpu.make_async_copy(src, dst, in_sem.at[2 * chunks + i])
         loads[name].start()
 
-    def sems(scan, phase, c):
-        return (scan * 3 + phase) * chunks + c
-
-    def send(scan, phase, c, source, landing, to):
-        at = sems(scan, phase, c)
-        pltpu.make_async_remote_copy(
-            src_ref=source,
-            dst_ref=landing,
-            send_sem=send_sem.at[at],
-            recv_sem=recv_sem.at[at],
-            device_id=(to, head),
+    def near(scan, phase, h):
+        return (scan * 2 + phase) * heads + h
+
+    def send_near(scan, phase, h, source, landing):
+        for p in near_partners:
+            pltpu.make_async_remote_copy(
+                src_ref=source.at[scan, h, p],
+                dst_ref=landing.at[scan, h, member],
+                send_sem=send_sem.at[near(scan, phase, h)],
+                recv_sem=recv_sem.at[near(scan, phase, h)],
+                device_id=(group * GROUP + p, head),
+                device_id_type=MESH,
+            ).start()
+        landing[scan, h, member] = source[scan, h, member]
+
+    def wait_near(sem, scan, phase, h):
+        view = gathered.at[scan, h, pl.ds(0, GROUP - 1)]
+        pltpu.make_async_copy(view, view, sem.at[near(scan, phase, h)]).wait()
+
+    def ahead(scan, p):
+        return p > group if scan == 0 else p < group
+
+    def far_send(scan, h, i):
+        p = far_partners[i]
+        return pltpu.make_async_remote_copy(
+            src_ref=here.at[scan, h],
+            dst_ref=totals.at[scan, h, group],
+            send_sem=far_send_sem.at[(scan * heads + h) * (n_group - 1) + i],
+            recv_sem=far_recv_sem.at[(scan * heads + h) * n_group + group],
+            device_id=(p * GROUP + member, head),
             device_id_type=MESH,
-        ).start()
-
-    def wait_for(sem, scan, phase, c):
-        n = (n_group if phase == 1 else GROUP) - 1
-        view = gathered.at[scan, c, pl.ds(0, n)]
-        pltpu.make_async_copy(view, view, sem.at[sems(scan, phase, c)]).wait()
-
-    def wait_exchange(scan, phase, c):
-        wait_for(recv_sem, scan, phase, c)
-
-    def wait_sent(scan, phase, c):
-        wait_for(send_sem, scan, phase, c)
-
-    def scatter(scan, c):
-        landing = gathered.at[scan, c, member]
-        for p in near_partners:
-            send(scan, 0, c, local.at[scan, c, p], landing, group * GROUP + p)
-        gathered[scan, c, member] = local[scan, c, member]
-
-    def share_totals(scan, c):
-        wait_exchange(scan, 0, c)
+        )
+
+    def scatter(scan, h):
+        send_near(scan, 0, h, local, gathered)
+
+    def share_totals(scan, h):
+        wait_near(recv_sem, scan, 0, h)
         sum_here = jnp.zeros((SLICE, HD), F32)
         for j in range(GROUP) if scan == 0 else range(GROUP - 1, -1, -1):
-            prefix[scan, c, j] = sum_here
-            sum_here = sum_here + gathered[scan, c, j]
-        totals[scan, c, group] = sum_here
-        mine = totals.at[scan, c, group]
-        for p in far_partners:
-            send(scan, 1, c, mine, mine, p * GROUP + member)
-
-    def hand_back(scan, c):
-        wait_exchange(scan, 1, c)
+            prefix[scan, h, j] = sum_here
+            sum_here = sum_here + gathered[scan, h, j]
+        here[scan, h] = sum_here
+        if scan == 0 and h == 0:
+
+            @pl.when(group < n_group - 1)
+            def _():
+                pl.semaphore_wait(entered, n_group - 1 - group)
+
+        for i, p in enumerate(far_partners):
+
+            @pl.when(ahead(scan, p))
+            def _():
+                far_send(scan, h, i).start()
+
+    def hand_back(scan, h):
         outside = jnp.zeros((SLICE, HD), F32)
         for j in range(n_group):
-            counts = j < group if scan == 0 else j > group
-            outside = outside + jnp.where(counts, totals[scan, c, j], 0.0)
+
+            @pl.when(group > j if scan == 0 else group < j)
+            def _():
+                view = totals.at[scan, h, j]
+                sem = far_recv_sem.at[(scan * heads + h) * n_group + j]
+                pltpu.make_async_copy(view, view, sem).wait()
+
+        for j in range(n_group):
+            outside = outside + totals[scan, h, j]
         for j in range(GROUP):
-            prefix[scan, c, j] = prefix[scan, c, j] + outside
-        landing = arrived.at[scan, c, member]
-        for p in near_partners:
-            send(scan, 2, c, prefix.at[scan, c, p], landing, group * GROUP + p)
-        arrived[scan, c, member] = prefix[scan, c, member]
+            prefix[scan, h, j] = prefix[scan, h, j] + outside
+        send_near(scan, 1, h, prefix, arrived)
+
+    def wait_sent(scan, h):
+        for phase in range(2):
+            wait_near(send_sem, scan, phase, h)
+        for i, p in enumerate(far_partners):
+
+            @pl.when(ahead(scan, p))
+            def _():
+                far_send(scan, h, i).wait_send()
 
     def place_states(scan, c, b, plain):
-        per = HD // SLICE
         for i in range(2):
             at = slice(i * HD, (i + 1) * HD)
-            s = arrived[scan, c, i * per : (i + 1) * per].reshape(HD, HD)
-            s = s if plain else s + first[scan, c, i]
+            s = arrived[scan, 2 * c + i].reshape(HD, HD)
+            s = s if plain else s + first[scan, 2 * c + i]
             pair[scan, c, b, at, at] = s.astype(BF16)
 
-    def outer_products(scan, c, product_of, keep):
-        for i in range(2):
-            h = 2 * c + i
-            parts = [product_of(h, b) for b in range(blocks)]
-            first[scan, c, i] = parts[keep]
-            per = HD // SLICE
-            local[scan, c, i * per : (i + 1) * per] = (parts[0] + parts[1]).reshape(
-                per, SLICE, HD
-            )
+    def outer_products(scan, h, product_of, keep):
+        parts = [product_of(h, b) for b in range(blocks)]
+        first[scan, h] = parts[keep]
+        local[scan, h] = sum(parts[1:], parts[0]).reshape(GROUP, SLICE, HD)
 
     def tile(h, b):
         return slice(b * BLK, (b + 1) * BLK), slice(h * HD, (h + 1) * HD)
@@ -228,13 +255,22 @@
         return dot(q_t[lane, row], dn[row, lane], NN)
 
     pair[...] = jnp.zeros_like(pair)
+    totals[...] = jnp.zeros_like(totals)
     for c in range(chunks):
         loads["k", c].wait()
         loads["v", c].wait()
-        outer_products(0, c, kv_product, 0)
-        if c == 0:
-            pl.semaphore_wait(barrier, n_group + GROUP + n_head - 3)
-        scatter(0, c)
+        for i in range(2):
+            outer_products(0, 2 * c + i, kv_product, 0)
+    pl.semaphore_wait(barrier, GROUP + n_head - 2 + group)
+    for p in far_partners:
+
+        @pl.when(p < group)
+        def _():
+            to = (p * GROUP + member, head)
+            pl.semaphore_signal(entered, inc=1, device_id=to, device_id_type=MESH)
+
+    for h in range(heads):
+        scatter(0, h)
 
     loads["q"].wait()
 
@@ -256,11 +292,11 @@
         return 0
 
     lax.fori_loop(0, heads * blocks // 2, scores, 0)
-    for c in range(chunks):
-        share_totals(0, c)
+    for h in range(heads):
+        share_totals(0, h)
     lax.fori_loop(heads * blocks // 2, heads * blocks, scores, 0)
-    for c in range(chunks):
-        hand_back(0, c)
+    for h in range(heads):
+        hand_back(0, h)
 
     loads["g"].wait()
     loads["gain"].wait()
@@ -268,7 +304,8 @@
     square = [None] * blocks
     product = [None] * blocks
     for c in range(chunks):
-        wait_exchange(0, 2, c)
+        for i in range(2):
+            wait_near(recv_sem, 0, 1, 2 * c + i)
         for b in range(blocks):
             place_states(0, c, b, b == 0)
             for i in range(2):
@@ -317,13 +354,12 @@
         for b in range(blocks)
     ]
 
-    for c in range(chunks):
-        for i in range(2):
-            for b in range(blocks):
-                at = tile(2 * c + i, b)
-                dn[at] = (ratios[b] * (gn[at] - weights[b] * num[at])).astype(BF16)
-        outer_products(1, c, qd_product, 1)
-        scatter(1, c)
+    for h in range(heads):
+        for b in range(blocks):
+            at = tile(h, b)
+            dn[at] = (ratios[b] * (gn[at] - weights[b] * num[at])).astype(BF16)
+        outer_products(1, h, qd_product, 1)
+        scatter(1, h)
 
     for h in range(heads):
         for b in range(blocks):
@@ -351,15 +387,16 @@
 
     steps = heads * blocks
     lax.fori_loop(0, 3 * steps // 8, backward, 0)
+    for h in range(heads):
+        share_totals(1, h)
+    lax.fori_loop(3 * steps // 8, 6 * steps // 8, backward, 0)
+    for h in range(heads):
+        hand_back(1, h)
+    lax.fori_loop(6 * steps // 8, steps, backward, 0)
+
     for c in range(chunks):
-        share_totals(1, c)
-    lax.fori_loop(3 * steps // 8, 6 * steps // 8, backward, 0)
-    for c in range(chunks):
-        hand_back(1, c)
-    lax.fori_loop(6 * steps // 8, steps, backward, 0)
-
-    for c in range(chunks):
-        wait_exchange(1, 2, c)
+        for i in range(2):
+            wait_near(recv_sem, 1, 1, 2 * c + i)
         for b in range(blocks):
             place_states(1, c, b, b == blocks - 1)
             if c < chunks - 1:
@@ -371,9 +408,8 @@
                 later[b] = pair[1, c, b]
 
     for scan in range(2):
-        for phase in range(3):
-            for c in range(chunks):
-                wait_sent(scan, phase, c)
+        for h in range(heads):
+            wait_sent(scan, h)
     stat_wait(stat_send)
 
 
@@ -428,7 +464,7 @@
     anywhere = pl.BlockSpec(memory_space=pl.ANY)
     big = pltpu.VMEM((rows, columns), BF16)
     wide = pltpu.VMEM((rows, columns), F32)
-    pieces = pltpu.VMEM((2, chunks, GROUP, SLICE, HD), F32)
+    pieces = pltpu.VMEM((2, heads, GROUP, SLICE, HD), F32)
     flops = heads * blocks * (12 * BLK * BLK * HD + 12 * BLK * HD * HD)
     vmem = pl.BlockSpec(memory_space=pltpu.VMEM)
     hbm = [
@@ -459,7 +495,7 @@
             pltpu.VMEM((columns, rows), BF16),
             wide,
             big,
-            pltpu.VMEM((2, chunks, 2, HD, HD), F32),
+            pltpu.VMEM((2, heads, HD, HD), F32),
             pieces,
             pltpu.VMEM((heads, blocks, HD, HD), BF16),
             pltpu.VMEM((2, chunks, blocks, 2 * HD, 2 * HD), BF16),
@@ -467,12 +503,16 @@
             pieces,
             pieces,
             pieces,
-            pltpu.VMEM((2, chunks, n_seq // GROUP, SLICE, HD), F32),
+            pltpu.VMEM((2, heads, SLICE, HD), F32),
+            pltpu.VMEM((2, heads, n_seq // GROUP, SLICE, HD), F32),
             pltpu.VMEM((2 * blocks, BLK), F32),
             pltpu.VMEM((n_head, 2 * blocks, BLK), F32),
             pltpu.SemaphoreType.DMA((2 * chunks + 3,)),
-            pltpu.SemaphoreType.DMA((6 * chunks,)),
-            pltpu.SemaphoreType.DMA((6 * chunks,)),
+            pltpu.SemaphoreType.DMA((4 * heads,)),
+            pltpu.SemaphoreType.DMA((4 * heads,)),
+            pltpu.SemaphoreType.DMA((2 * heads * (n_seq // GROUP - 1),)),
+            pltpu.SemaphoreType.DMA((2 * heads * (n_seq // GROUP),)),
+            pltpu.SemaphoreType.REGULAR,
             pltpu.SemaphoreType.DMA,
             pltpu.SemaphoreType.DMA,
         ],

time: 45.5 us -> 43.8 us (0.963)
  Pallas kernels: 44.8 us -> 43.1 us
    pallas_call x1, Pallas kernels: 42.7 us -> 41 us  [shards(): pl.pallas_call(functools.partial(kernel, n_seq, n_head, columns * n_head)...]
where the time goes in v5:
time: 43.8 us; the launch traced here: 43.7 us
  Pallas kernels  43.1 us (98%)
  between operations  0.64 us (1%)
    pallas_call x1, Pallas kernels, shards(): pl.pallas_call(functools.partial(kernel, n_seq, n_head, columns * n_head)...  41 us
    pallas_call x1, Pallas kernels, shards(): pl.pallas_call(finish, out_shape=(out, out, out, out), in_specs=[vmem] *...  2.08 us

profile of v5, /device:TPU:2, one launch (start us, length us, event | category | flops | bytes accessed | tf_op | source)
XLA Modules:
  0.0 43.7 jit_solution(8914536998420246546)
XLA Ops:
  0.6 41.0 %shard_map.84 = (bf16[1024,512]{1,0:T(8,128)(2,1)S(1)}, bf16[1024,512]{1,0:T(8,128)(2,1)S(1)}, bf16[1024,512]{1,0:T(8,128)(2,1)S(1)}, bf16[1024,512]{1,0:T(8,128...) custom-call(bf16[1024,512]{1,0:T(8,128)(2,1)} %q_hbm.1, ...), custom_call_target="tpu_custom_call" | custom-call | flops 4026531840 | bytes 4194304 | tf_op jit(solution)/shard_map/pallas_call | solution.py:485
  41.7 2.1 %shard_map.85 = (bf16[1024,512]{1,0:T(8,128)(2,1)}, bf16[1024,512]{1,0:T(8,128)(2,1)}, bf16[1024,512]{1,0:T(8,128)(2,1)}, bf16[1024,512]{1,0:T(8,128)(2,1)}) custom-call(bf16[1024,512]{1,0:T(8,128)(2,1)S(1)} %get-tuple-element.13.normed, bf16[1024,512]{1,0:T(8,128)(2,1)S(1)} %get-tuple-element.14.gq, bf16[1024,512]{1,0:T(8,128)(2,1)S(1)} %get-tuple-element.15.gk_done, ...), custom_call_target="tpu_custom_call" | custom-call | flops 268435456 | bytes 4194304 | tf_op jit(solution)/shard_map/pallas_call | solution.py:526

commit v6 on v5

--- a/solution.py
+++ b/solution.py
@@ -395,6 +395,11 @@
     lax.fori_loop(6 * steps // 8, steps, backward, 0)
 
     for c in range(chunks):
+        if c == chunks - 1:
+            for scan in range(2):
+                for h in range(heads):
+                    wait_sent(scan, h)
+            stat_wait(stat_send)
         for i in range(2):
             wait_near(recv_sem, 1, 1, 2 * c + i)
         for b in range(blocks):
@@ -406,11 +411,6 @@
                 )
             else:
                 later[b] = pair[1, c, b]
-
-    for scan in range(2):
-        for h in range(heads):
-            wait_sent(scan, h)
-    stat_wait(stat_send)
 
 
 def finish(

time: 43.8 us -> 43.8 us (level)
  no operation moved by 1% of the time
where the time goes in v6:
time: 43.8 us; the launch traced here: 43.7 us
  Pallas kernels  43 us (98%)
  between operations  0.64 us (1%)
    pallas_call x1, Pallas kernels, shards(): pl.pallas_call(functools.partial(kernel, n_seq, n_head, columns * n_head)...  41 us
    pallas_call x1, Pallas kernels, shards(): pl.pallas_call(finish, out_shape=(out, out, out, out), in_specs=[vmem] *...  2.08 us

profile of v6, /device:TPU:2, one launch (start us, length us, event | category | flops | bytes accessed | tf_op | source)
XLA Modules:
  0.0 43.7 jit_solution(658907320989349285)
XLA Ops:
  0.6 41.0 %shard_map.84 = (bf16[1024,512]{1,0:T(8,128)(2,1)S(1)}, bf16[1024,512]{1,0:T(8,128)(2,1)S(1)}, bf16[1024,512]{1,0:T(8,128)(2,1)S(1)}, bf16[1024,512]{1,0:T(8,128...) custom-call(bf16[1024,512]{1,0:T(8,128)(2,1)} %q_hbm.1, ...), custom_call_target="tpu_custom_call" | custom-call | flops 4026531840 | bytes 4194304 | tf_op jit(solution)/shard_map/pallas_call | solution.py:485
  41.6 2.1 %shard_map.85 = (bf16[1024,512]{1,0:T(8,128)(2,1)}, bf16[1024,512]{1,0:T(8,128)(2,1)}, bf16[1024,512]{1,0:T(8,128)(2,1)}, bf16[1024,512]{1,0:T(8,128)(2,1)}) custom-call(bf16[1024,512]{1,0:T(8,128)(2,1)S(1)} %get-tuple-element.13.normed, bf16[1024,512]{1,0:T(8,128)(2,1)S(1)} %get-tuple-element.14.gq, bf16[1024,512]{1,0:T(8,128)(2,1)S(1)} %get-tuple-element.15.gk_done, ...), custom_call_target="tpu_custom_call" | custom-call | flops 268435456 | bytes 4194304 | tf_op jit(solution)/shard_map/pallas_call | solution.py:526
